TPU v7x, 256 devices: a whole 4x4x8 slice. The times are simulated.
256 devices in a mesh: dp: 16 (over x, y), seq: 16 (over z, core).
Axes of the slice: x: 4, y: 4, z: 8, core: 2. Of those that a mesh axis runs over, the one named last changes fastest.
Arguments:
- features: bfloat16 [128, 32, 32, 512], P('dp', 'seq'), may hold values from -6 to 6
- conv_weight: bfloat16 [3, 3, 3, 16, 512], replicated, may hold values from -0.0546875 to 0.0546875
- clip_frames: int32 [32], replicated, may hold values from 1 to 7, as said below
- clip_group: int32 [32], replicated, may hold values from 0 to 15, as said below
- clip_offset: int32 [32], replicated, may hold values from 0 to 7, as said below
- clip_times: float32 [32], replicated, may hold values from 0.05 to 0.95
- noise_tokens: bfloat16 [16, 2048, 64], P('dp', 'seq'), may hold values from -6 to 6
- embed_weight: bfloat16 [64, 2048], replicated, may hold values from -0.75 to 0.75
- attention_proj: bfloat16 [2048, 3, 16, 128], P(None, None, 'seq'), may hold values from -0.125 to 0.125
- norm_gains: float32 [2, 128], replicated, may hold values from 0.5 to 1.5
- cotangent: bfloat16 [16, 2048, 2048], P('dp', 'seq'), may hold values from -0.03125 to 0.03125
Outputs:
- noisy_tokens: float32 [16, 2048, 64], P('dp', 'seq')
- attention_out: bfloat16 [16, 2048, 2048], P('dp', 'seq')
- proj_grad: float32 [2048, 3, 16, 128], P('dp', None, 'seq')
- norm_grad: float32 [2, 128], replicated
Inputs may be any that keep to these rules, and one draw needn't show every extreme that they name: `clip_frames`: clips follow one another along time from frame 0 and together cover all 128 frames. `clip_group`: every group trains on exactly two clips, whose frames add up to 8. `clip_offset`: the clips of one group take consecutive frame slots from slot 0 in their time order and fill all 8 slots of the group.
All inputs are finite; a program needn't handle non-finite values.
Results may differ from a plain program's by a relative error of at most 0.014.
Values may be sent and summed in bfloat16 or wider, within the bound.
A program may use at most 128 MiB of HBM per device.

v0:
```python
import jax
import jax.numpy as jnp
from jax import lax
from jax.sharding import PartitionSpec as P


def shifted(block, axis, distance):
    devices = range(lax.axis_size(axis))
    route = [(i - distance, i) for i in devices if i - distance in devices]
    return lax.ppermute(block, axis, route)


def padded_2(array, sides, width):
    for axis, dim in sides:
        peers, length = (lax.axis_size(axis), array.shape[dim])
        up = [(i, (i + 1) % peers) for i in range(peers - 1)]
        down = [(j, i) for i, j in up]
        last = lax.slice_in_dim(array, length - width, length, axis=dim)
        first = lax.slice_in_dim(array, 0, width, axis=dim)
        before = lax.ppermute(last, axis, up)
        after = lax.ppermute(first, axis, down)
        array = jnp.concatenate([before, array, after], axis=dim)
    return array


def clip_bounds(clip_frames):
    ends_at = jnp.cumsum(clip_frames)
    return (ends_at - clip_frames, ends_at)


def frame_start(frame_ids, starts_at, ends_at):
    member = (frame_ids[:, None] >= starts_at[None, :]) & (frame_ids[:, None] < ends_at[None, :])
    own_start = jnp.sum(jnp.where(member, starts_at[None, :], 0), axis=1)
    return (own_start, member)


def slot_table(group_id, slot_ids, clip_group, clip_offset, clip_frames, starts_at, clip_times):
    member = (
        (clip_group[None, :] == group_id)
        & (slot_ids[:, None] >= clip_offset[None, :])
        & (slot_ids[:, None] < clip_offset[None, :] + clip_frames[None, :])
    )
    numbers = jnp.arange(clip_frames.shape[0])
    usable = jnp.any(member, axis=1).astype(jnp.float32)
    segment = jnp.sum(jnp.where(member, numbers[None, :] + 1, 0), axis=1) - 1
    source = jnp.sum(
        jnp.where(member, starts_at[None, :] + slot_ids[:, None] - clip_offset[None, :], 0), axis=1
    )
    noise_level = jnp.sum(
        jnp.where(member, clip_times[None, :], jnp.zeros((), clip_times.dtype)), axis=1
    )
    return (usable, segment, source, noise_level)


def rms_scale(values, gain_row):
    inverse = lax.rsqrt(jnp.mean(values * values, axis=-1, keepdims=True) + 1e-06)
    return (values * inverse * gain_row, inverse)


def rms_back(values, inverse, gain_row, upstream):
    scaled = gain_row * upstream
    grad_in = inverse * scaled - values * inverse**3 * jnp.mean(
        values * scaled, axis=-1, keepdims=True
    )
    gain_part = jnp.sum(upstream * values * inverse, axis=(0, 1))
    return (grad_in, gain_part)


def body(
    features,
    conv_weight,
    clip_frames,
    clip_group,
    clip_offset,
    clip_times,
    noise_tokens,
    embed_weight,
    attention_proj,
    norm_gains,
    cotangent,
):
    slab_id = lax.axis_index("dp")
    groups_n = lax.axis_size("dp")
    seq_n = lax.axis_size("seq")
    frames_dev = features.shape[0]
    width_n = features.shape[2]
    channels = features.shape[3]
    tokens_row = width_n // 2
    tok_dev = noise_tokens.shape[1]
    patch_ch = noise_tokens.shape[2]
    latent_ch = conv_weight.shape[3]
    starts_at, ends_at = clip_bounds(clip_frames)
    local_ids = jnp.arange(frames_dev)
    frame_ids = slab_id * frames_dev + local_ids
    own_start, member = frame_start(frame_ids, starts_at, ends_at)
    activated = jax.nn.silu(features.astype(jnp.float32)).astype(jnp.bfloat16)
    before = shifted(activated[frames_dev - 2 :], "dp", 1)
    extended = jnp.concatenate([before, activated], axis=0)
    rimmed = padded_2(extended, (("seq", 1),), 1)
    padded = jnp.pad(rimmed, ((0, 0), (0, 0), (1, 1), (0, 0)))
    voxels = frames_dev * 2 * width_n
    latent = jnp.zeros((latent_ch, voxels), jnp.float32)
    for tap_time in range(3):
        allowed = (frame_ids - (2 - tap_time) >= own_start).astype(jnp.float32)
        allowed_cols = jnp.repeat(allowed, 2 * width_n)[None, :]
        for tap_row in range(3):
            for tap_col in range(3):
                tap_piece = padded[
                    tap_time : tap_time + frames_dev,
                    tap_row : tap_row + 2,
                    tap_col : tap_col + width_n,
                ].reshape(voxels, channels)
                tap_term = lax.dot_general(
                    conv_weight[tap_time, tap_row, tap_col],
                    tap_piece,
                    (((1,), (1,)), ((), ())),
                    preferred_element_type=jnp.float32,
                )
                latent = latent + allowed_cols * tap_term
    patches = (
        latent.reshape(latent_ch, frames_dev, 2, tokens_row, 2)
        .transpose(1, 3, 2, 4, 0)
        .reshape(frames_dev, tokens_row, patch_ch)
    )
    usable, segment, source, noise_level = slot_table(
        slab_id, local_ids, clip_group, clip_offset, clip_frames, starts_at, clip_times
    )
    target = jnp.sum(
        jnp.where(
            member,
            clip_group[None, :] * frames_dev
            + clip_offset[None, :]
            + frame_ids[:, None]
            - starts_at[None, :],
            0,
        ),
        axis=1,
    )
    inclip = jnp.any(member, axis=1)
    slot_all = jnp.arange(groups_n * frames_dev)
    placement = ((target[:, None] == slot_all[None, :]) & inclip[:, None]).astype(jnp.float32)
    placed = jnp.einsum("fs,fcj->scj", placement, patches, precision=lax.Precision.HIGHEST).reshape(
        groups_n, frames_dev, tokens_row, patch_ch
    )
    arrived = lax.psum_scatter(placed, "dp", scatter_dimension=0, tiled=True)[0]
    noise_slots = noise_tokens.reshape(frames_dev, tokens_row, patch_ch).astype(jnp.float32)
    noisy_slots = usable[:, None, None] * (
        (1.0 - noise_level[:, None, None]) * arrived + noise_level[:, None, None] * noise_slots
    )
    noisy_out = noisy_slots.reshape(1, tok_dev, patch_ch)
    token_bf = noisy_slots.reshape(tok_dev, patch_ch).astype(jnp.bfloat16)
    local_hidden = jnp.dot(token_bf, embed_weight, preferred_element_type=jnp.float32).astype(
        jnp.bfloat16
    )
    hidden = lax.all_gather(local_hidden, "seq", axis=0, tiled=True)
    seq_len = hidden.shape[0]
    model_n = attention_proj.shape[0]
    heads_dev = attention_proj.shape[2]
    head_dim = attention_proj.shape[3]
    mixed_all = jnp.dot(
        hidden,
        attention_proj.reshape(model_n, 3 * heads_dev * head_dim),
        preferred_element_type=jnp.float32,
    ).reshape(seq_len, 3, heads_dev, head_dim)
    query_n, query_inv = rms_scale(mixed_all[:, 0], norm_gains[0])
    key_n, key_inv = rms_scale(mixed_all[:, 1], norm_gains[1])
    query_bf = query_n.astype(jnp.bfloat16)
    key_bf = key_n.astype(jnp.bfloat16)
    value_bf = mixed_all[:, 2].astype(jnp.bfloat16)
    cot_rows = cotangent.reshape(tok_dev, seq_n * heads_dev, head_dim)
    incoming = lax.all_to_all(cot_rows, "seq", split_axis=1, concat_axis=0, tiled=True)
    token_usable = jnp.tile(jnp.repeat(usable, tokens_row), seq_n)
    token_seg = jnp.tile(jnp.repeat(segment, tokens_row), seq_n)
    incoming = jnp.where(token_usable[:, None, None] > 0, incoming, jnp.zeros((), jnp.bfloat16))
    score_scale = head_dim ** (-0.5)
    block_n = min(512, seq_len)
    block_count = seq_len // block_n

    def block_step(running, inputs):
        key_grad, value_grad = running
        query_blk, grad_blk, seg_blk, keep_blk = inputs
        scores = (
            jnp.einsum("bhe,she->hbs", query_blk, key_bf, preferred_element_type=jnp.float32)
            * score_scale
        )
        same_clip = seg_blk[:, None] == token_seg[None, :]
        exp_scores = jnp.where(same_clip[None], jnp.exp(scores), 0.0)
        prob_rows = exp_scores / jnp.sum(exp_scores, axis=2, keepdims=True)
        probs_bf = prob_rows.astype(jnp.bfloat16)
        output = jnp.einsum("hbs,she->bhe", probs_bf, value_bf, preferred_element_type=jnp.float32)
        prob_grad = jnp.einsum(
            "bhe,she->hbs", grad_blk, value_bf, preferred_element_type=jnp.float32
        )
        row_delta = jnp.sum(prob_rows * prob_grad, axis=2, keepdims=True)
        score_grad = (prob_rows * (prob_grad - row_delta) * score_scale).astype(jnp.bfloat16)
        query_grad = jnp.einsum(
            "hbs,she->bhe", score_grad, key_bf, preferred_element_type=jnp.float32
        )
        key_grad = key_grad + jnp.einsum(
            "hbs,bhe->she", score_grad, query_blk, preferred_element_type=jnp.float32
        )
        value_grad = value_grad + jnp.einsum(
            "hbs,bhe->she", probs_bf, grad_blk, preferred_element_type=jnp.float32
        )
        shown_rows = (keep_blk[:, None, None] * output).astype(jnp.bfloat16)
        return ((key_grad, value_grad), (shown_rows, query_grad))

    start_state = (
        jnp.zeros((seq_len, heads_dev, head_dim), jnp.float32),
        jnp.zeros((seq_len, heads_dev, head_dim), jnp.float32),
    )
    scan_inputs = (
        query_bf.reshape(block_count, block_n, heads_dev, head_dim),
        incoming.reshape(block_count, block_n, heads_dev, head_dim),
        token_seg.reshape(block_count, block_n),
        token_usable.reshape(block_count, block_n),
    )
    final_state, scan_out = lax.scan(block_step, start_state, scan_inputs)
    key_grad, value_grad = final_state
    shown_rows = scan_out[0].reshape(seq_len, heads_dev, head_dim)
    query_grad = scan_out[1].reshape(seq_len, heads_dev, head_dim)
    token_out = lax.all_to_all(shown_rows, "seq", split_axis=0, concat_axis=1, tiled=True).reshape(
        1, tok_dev, seq_n * heads_dev * head_dim
    )
    query_in, query_gain = rms_back(mixed_all[:, 0], query_inv, norm_gains[0], query_grad)
    key_in, key_gain = rms_back(mixed_all[:, 1], key_inv, norm_gains[1], key_grad)
    stacked = (
        jnp.stack([query_in, key_in, value_grad], axis=1)
        .astype(jnp.bfloat16)
        .reshape(seq_len, 3 * heads_dev * head_dim)
    )
    proj_term = lax.dot_general(
        hidden, stacked, (((0,), (0,)), ((), ())), preferred_element_type=jnp.float32
    ).reshape(model_n, 3, heads_dev, head_dim)
    proj_grad = lax.psum_scatter(
        proj_term.astype(jnp.bfloat16), "dp", scatter_dimension=0, tiled=True
    ).astype(jnp.float32)
    norm_grad = lax.psum(jnp.stack([query_gain, key_gain]), ("dp", "seq"))
    return (noisy_out, token_out, proj_grad, norm_grad)


def solution(mesh):
    return jax.shard_map(
        body,
        mesh=mesh,
        in_specs=(
            P("dp", "seq", None, None),
            P(),
            P(),
            P(),
            P(),
            P(),
            P("dp", "seq", None),
            P(),
            P(None, None, "seq", None),
            P(),
            P("dp", "seq", None),
        ),
        out_specs=(P("dp", "seq", None), P("dp", "seq", None), P("dp", None, "seq", None), P()),
        check_vma=False,
    )
```

profile of v0, /device:TPU:1, one launch (start us, length us, event | category | flops | bytes accessed | tf_op | source)
XLA Modules:
  0.0 380.5 jit_solution(9365460250757747422)
XLA Ops:
  8.7 4.0 %collective-permute-start = (bf16[2,2,32,512]{3,2,1,0:T(8,128)(2,1)S(1)}, bf16[2,2,32,512]{3,2,1,0:T(8,128)(2,1)S(1)}, u32[]{:S(2)}, u32[]{:S(2)}) collective-permute-start(bf16[2,2,32,512]{3,2,1,0:T(8,128)(2,1)S(1)} %slice.274), channel_id=1, source_target_pairs={{0,16},{16,32},{32,48},{48,64},{64,80},{80,96},{96,112},{112,128},... | collective-permute-start | bytes 393224 | tf_op jit(solution)/shard_map/ppermute | solution.py:10
  17.3 4.4 %collective-permute-start.1 = (bf16[10,1,32,512]{3,2,1,0:T(8,128)(2,1)S(1)}, bf16[10,1,32,512]{3,2,1,0:T(8,128)(2,1)S(1)}, u32[]{:S(2)}, u32[]{:S(2)}) collective-permute-start(bf16[10,1,32,512]{3,2,1,0:T(8,128)(2,1)S(1)} %get-tuple-element.273), channel_id=1, source_target_pairs={{0,1},{1,2},{2,3},{3,4},{4,5},{5,6},{6,7},{7,8},{8,9},{9,10},{10,1... | collective-permute-start | bytes 983048 | tf_op jit(solution)/shard_map/ppermute | solution.py:20
  25.7 4.4 %collective-permute-done.2 = bf16[10,1,32,512]{3,2,1,0:T(8,128)(2,1)S(1)} collective-permute-done((bf16[10,1,32,512]{3,2,1,0:T(8,128)(2,1)S(1)}, bf16[10,1,32,512]{3,2,1,0:T(8,128)(2,1)S(1)}, u32[]{:S(2)}, u32[]{:S(2)}) %collective-permute-start.2) | collective-permute-done | bytes 327712 | tf_op jit(solution)/shard_map/ppermute | solution.py:21
  31.8 3.3 fusion.178
  44.7 77.8 %reduce-scatter.7.cloned.1.call-done = f32[1,8,16,64]{3,2,1,0:T(8,128)} async-done(((f32[16,8,16,64]{3,2,1,0:T(8,128)}), f32[1,8,16,64]{3,2,1,0:T(8,128)}) %reduce-scatter.7.cloned.1.call-update) | async-done | bytes 32784
  125.6 9.3 %all-to-all-start = ((bf16[128,16,128]{0,2,1:T(8,128)(2,1)}), bf16[128,16,128]{0,2,1:T(8,128)(2,1)S(1)}, u32[]{:S(2)}, u32[]{:S(2)}) async-start(bf16[128,16,128]{0,2,1:T(8,128)(2,1)} %bitcast.88), calls=%async_computation | async-start | bytes 1048576 | tf_op jit(solution)/shard_map/all_to_all | solution.py:171
  137.8 18.9 %all-to-all-done = bf16[128,16,128]{0,2,1:T(8,128)(2,1)S(1)} async-done(((bf16[128,16,128]{0,2,1:T(8,128)(2,1)}), bf16[128,16,128]{0,2,1:T(8,128)(2,1)S(1)}, u32[]{:S(2)}, u32[]{:S(2)}) %all-to-all-start) | async-done | bytes 524320 | tf_op jit(solution)/shard_map/all_to_all | solution.py:171
  158.0 33.4 %all-gather.2.cloned.1.call-done = bf16[2048,2048]{1,0:T(8,128)(2,1)} async-done(((bf16[128,2048]{1,0:T(8,128)(2,1)}), bf16[2048,2048]{1,0:T(8,128)(2,1)}) %all-gather.2.cloned.1.call-update) | async-done | bytes 8388624 | tf_op jit(solution)/shard_map/all_gather | solution.py:155
  191.3 6.3 %fusion.30 = f32[2048,3,128]{0,2,1:T(8,128)S(1)} fusion(bf16[2048,2048]{1,0:T(8,128)(2,1)} %all-gather.2.cloned.1.call-done, bf16[2048,3,1,128]{0,3,1,2:T(8,128)(2,1)} %copy.117), kind=kOutput, calls=%fused_computation.40 | convolution fusion | flops 3221225472 | bytes 13107200 | tf_op jit(solution)/shard_map/dot_general | solution.py:160
  206.2 62.1 %while.17 = (s32[]{:T(128)}, f32[2048,1,128]{0,2,1:T(8,128)S(1)}, f32[2048,1,128]{0,2,1:T(8,128)}, bf16[4,512,1,128]{3,1,2,0:T(8,128)(2,1)}, f32[4,512,1,128]{3,...) while((s32[]{:T(128)}, f32[2048,1,128]{0,2,1:T(8,128)S(1)}, ...), condition=%wide.region_13.14_spmd.clone, body=%wide.region_10.13_spmd.clone.sunk | while | flops 1628568576 | bytes 76458728 | solution.py:218
  206.2 2.3 fusion.234
  208.5 2.5 multiply_reduce_fusion.5
  214.1 2.4 fusion.236
  216.5 2.5 fusion.237
  219.0 2.5 fusion.238
  221.5 2.3 fusion.234
  223.8 2.5 multiply_reduce_fusion.5
  229.3 2.8 fusion.236
  232.2 2.5 fusion.237
  234.6 2.4 fusion.238
  237.1 2.3 fusion.234
  239.4 2.5 multiply_reduce_fusion.5
  244.9 2.8 fusion.236
  247.8 2.5 fusion.237
  250.3 2.5 fusion.238
  255.0 2.5 multiply_reduce_fusion.5
  260.6 2.8 fusion.236
  263.4 2.5 fusion.237
  265.9 2.5 fusion.238
  278.5 8.1 %fusion.36 = bf16[2048,3,1,128]{3,0,1,2:T(8,128)(2,1)} fusion(bf16[2048,2048]{1,0:T(8,128)(2,1)} %all-gather.2.cloned.1.call-done, bf16[2048,1,1,128]{0,3,2,1:T(8,128)(2,1)S(1)} %copy-done.8, bf16[2048,1,1,128]{0,3,2,1:T(8,128)(2,1)S(1)} %fusion.89, bf16[2048,1,1,128]{0,3,2,1:T(8,128)(2,1)S(1)} %subtract_convert_fusion.1), kind=kOutput, calls=%fused_computation.46 | convolution fusion | flops 3226730496 | bytes 11534336 | tf_op jit(solution)/shard_map/dot_general | solution.py:232
  289.1 4.8 %all-to-all-start.1 = ((bf16[16,2,8192]{2,1,0:T(2,128)(2,1)}), bf16[16,2,8192]{2,1,0:T(2,128)(2,1)S(1)}, u32[]{:S(2)}, u32[]{:S(2)}) async-start(bf16[16,2,8192]{2,1,0:T(2,128)(2,1)} %reshape.833), calls=%async_computation.1 | async-start | bytes 1048576 | tf_op jit(solution)/shard_map/all_to_all | solution.py:222
  294.7 75.7 %psum.7 = f32[2,128]{1,0:T(2,128)} all-reduce(f32[2,128]{1,0:T(2,128)S(1)} %pad_maximum_fusion.2), channel_id=1, replica_groups=mesh['dp'=16,'seq'=16] {'dp','seq'}, use_global_device_ids=true, to_apply=%region_19.20 | all-reduce | flops 256 | bytes 2048 | tf_op jit(solution)/shard_map/psum | solution.py:238
  (192 shorter events, 68.2 us)
Async XLA Ops:
  7.2 116.2 %copy-start = (bf16[64,2048]{1,0:T(8,128)(2,1)S(1)}, bf16[64,2048]{1,0:T(8,128)(2,1)}, u32[]{:S(2)}) copy-start(bf16[64,2048]{1,0:T(8,128)(2,1)} %param.20) | copy-start | bytes 786436
  7.2 16.5 %copy-start.10 = (bf16[3,3,3,16,512]{4,3,2,1,0:T(8,128)(2,1)S(1)}, bf16[3,3,3,16,512]{4,3,2,1,0:T(8,128)(2,1)}, u32[]{:S(2)}) copy-start(bf16[3,3,3,16,512]{4,3,2,1,0:T(8,128)(2,1)} %param.14) | copy-start | bytes 1327108
  7.2 115.3 %reduce-scatter.7.cloned.1.call-start = ((), (), s32[]{:S(2)}) async-start(), calls=%async_computation.6 | async-start | bytes 1114112
  8.7 8.5 %collective-permute-start = (bf16[2,2,32,512]{3,2,1,0:T(8,128)(2,1)S(1)}, bf16[2,2,32,512]{3,2,1,0:T(8,128)(2,1)S(1)}, u32[]{:S(2)}, u32[]{:S(2)}) collective-permute-start(bf16[2,2,32,512]{3,2,1,0:T(8,128)(2,1)S(1)} %slice.274), channel_id=1, source_target_pairs={{0,16},{16,32},{32,48},{48,64},{64,80},{80,96},{96,112},{112,128},... | collective-permute-start | bytes 393224 | tf_op jit(solution)/shard_map/ppermute | solution.py:10
  17.3 8.4 %collective-permute-start.1 = (bf16[10,1,32,512]{3,2,1,0:T(8,128)(2,1)S(1)}, bf16[10,1,32,512]{3,2,1,0:T(8,128)(2,1)S(1)}, u32[]{:S(2)}, u32[]{:S(2)}) collective-permute-start(bf16[10,1,32,512]{3,2,1,0:T(8,128)(2,1)S(1)} %get-tuple-element.273), channel_id=1, source_target_pairs={{0,1},{1,2},{2,3},{3,4},{4,5},{5,6},{6,7},{7,8},{8,9},{9,10},{10,1... | collective-permute-start | bytes 983048 | tf_op jit(solution)/shard_map/ppermute | solution.py:20
  21.7 8.4 %collective-permute-start.2 = (bf16[10,1,32,512]{3,2,1,0:T(8,128)(2,1)S(1)}, bf16[10,1,32,512]{3,2,1,0:T(8,128)(2,1)S(1)}, u32[]{:S(2)}, u32[]{:S(2)}) collective-permute-start(bf16[10,1,32,512]{3,2,1,0:T(8,128)(2,1)S(1)} %get-tuple-element.274), channel_id=1, source_target_pairs={{1,0},{2,1},{3,2},{4,3},{5,4},{6,5},{7,6},{8,7},{9,8},{10,9},{11,1... | collective-permute-start | bytes 983048 | tf_op jit(solution)/shard_map/ppermute | solution.py:21
  41.2 2.9 copy-start.13
  41.2 2.9 copy-start.15
  41.2 82.2 %copy-start.12 = (bf16[1,128,64]{1,2,0:T(8,128)(2,1)S(1)}, bf16[1,128,64]{1,2,0:T(8,128)(2,1)}, u32[]{:S(2)}) copy-start(bf16[1,128,64]{1,2,0:T(8,128)(2,1)} %param.19) | copy-start | bytes 49156
  41.7 82.8 %copy-start.9 = (bf16[1,128,2048]{2,1,0:T(8,128)(2,1)S(1)}, bf16[1,128,2048]{2,1,0:T(8,128)(2,1)}, u32[]{:S(2)}) copy-start(bf16[1,128,2048]{2,1,0:T(8,128)(2,1)} %param.23) | copy-start | bytes 1572868
  42.7 92.4 %copy-start.7 = (bf16[2048,3,1,128]{3,0,2,1:T(8,128)(2,1)S(1)}, bf16[2048,3,1,128]{3,0,2,1:T(8,128)(2,1)}, u32[]{:S(2)}) copy-start(bf16[2048,3,1,128]{3,0,2,1:T(8,128)(2,1)} %param.21) | copy-start | bytes 4718596
  44.0 147.3 %all-gather.2.cloned.1.call-start = ((), (), s32[]{:S(2)}) async-start(), calls=%async_computation.4 | async-start | bytes 8912896 | tf_op jit(solution)/shard_map/all_gather | solution.py:155
  124.5 13.3 %copy-start.14 = (f32[2,128]{1,0:T(2,128)S(1)}, f32[2,128]{1,0:T(2,128)}, u32[]{:S(2)}) copy-start(f32[2,128]{1,0:T(2,128)} %param.22) | copy-start | bytes 3076
  125.6 31.1 %all-to-all-start = ((bf16[128,16,128]{0,2,1:T(8,128)(2,1)}), bf16[128,16,128]{0,2,1:T(8,128)(2,1)S(1)}, u32[]{:S(2)}, u32[]{:S(2)}) async-start(bf16[128,16,128]{0,2,1:T(8,128)(2,1)} %bitcast.88), calls=%async_computation | async-start | bytes 1048576 | tf_op jit(solution)/shard_map/all_to_all | solution.py:171
  134.9 237.4 %reduce-scatter.5.cloned.1.call-start = ((), (), s32[]{:S(2)}) async-start(), calls=%async_computation.5 | async-start | bytes 1671168 | tf_op jit(solution)/shard_map/reduce_scatter | solution.py:235
  197.7 1.7 copy-start.4
  208.5 2.5 copy-start.2
  211.8 2.3 copy-start.3
  223.8 2.5 copy-start.2
  227.1 2.3 copy-start.3
  239.4 2.5 copy-start.2
  242.7 2.3 copy-start.3
  255.0 2.5 copy-start.2
  258.3 2.3 copy-start.3
  268.3 3.7 copy-start.5
  275.5 3.0 copy-start.8
  278.5 8.6 %copy-start.6 = (bf16[4,512,1,128]{3,1,2,0:T(8,128)(2,1)S(1)}, bf16[4,512,1,128]{3,1,2,0:T(8,128)(2,1)}, u32[]{:S(2)}) copy-start(bf16[4,512,1,128]{3,1,2,0:T(8,128)(2,1)} %get-tuple-element.69) | copy-start | bytes 1572868
  286.6 7.3 %copy-start.11 = (f32[1,8,16,64]{3,2,1,0:T(8,128)S(1)}, f32[1,8,16,64]{3,2,1,0:T(8,128)}, u32[]{:S(2)}) copy-start(f32[1,8,16,64]{3,2,1,0:T(8,128)} %reduce-scatter.7.cloned.1.call-done) | copy-start | bytes 98308
  288.2 85.8 %copy-start.1 = (bf16[64,2048]{1,0:T(8,128)(2,1)S(1)}, bf16[64,2048]{1,0:T(8,128)(2,1)}, u32[]{:S(2)}) copy-start(bf16[64,2048]{1,0:T(8,128)(2,1)} %param.20) | copy-start | bytes 786436
  289.1 81.2 %all-to-all-start.1 = ((bf16[16,2,8192]{2,1,0:T(2,128)(2,1)}), bf16[16,2,8192]{2,1,0:T(2,128)(2,1)S(1)}, u32[]{:S(2)}, u32[]{:S(2)}) async-start(bf16[16,2,8192]{2,1,0:T(2,128)(2,1)} %reshape.833), calls=%async_computation.1 | async-start | bytes 1048576 | tf_op jit(solution)/shard_map/all_to_all | solution.py:222
Sparse Core Ops, SparseCore 0:
  44.1 78.2 reduce-scatter.6
  124.7 66.6 all-gather.1
  286.8 73.5 reduce-scatter.4
where the time goes:
time: 382 us; the launch traced here: 380 us
  waiting for transfers between devices  136 us (36%)
  matrix products  79.2 us (21%)
  blocking collectives  75.7 us (20%)
  local copies, waits for them, and re-layouts  27.2 us (7%)
  starting transfers between devices  24.7 us (6%)
  other arithmetic  23 us (6%)
  between operations  14.3 us (4%)
    unnamed x4, waiting for transfers between devices  77.8 us
    psum x1, blocking collectives, body(): norm_grad = lax.psum(jnp.stack([query_gain, key_gain]), ('dp', 'seq'))  75.7 us
    all_gather x1, waiting for transfers between devices, body(): hidden = lax.all_gather(local_hidden, 'seq', axis=0, tiled=True)  33.4 us
    all_to_all x1, waiting for transfers between devices, body(): lax.all_to_all(cot_rows, 'seq', split_axis=1, concat_axis=0, tiled=True)  18.9 us
    unnamed x38, local copies, waits for them, and re-layouts  12.3 us
    dot_general x4, matrix products, block_step(): jnp.einsum('hbs,bhe->she', probs_bf, grad_blk, preferred_element_type=jnp...  11 us
    dot_general x4, matrix products, block_step(): jnp.einsum('bhe,she->hbs', grad_blk, value_bf, preferred_element_type=jnp...  9.98 us
    dot_general x4, matrix products, block_step(): jnp.einsum('hbs,she->bhe', probs_bf, value_bf, preferred_element_type=jnp...  9.88 us
  transfers between devices with their start and end apart: 8, of which 5 were waited for; matrix products, arithmetic and copies ran while one was open for 4% of the time, Pallas kernels for 0%

commit v1 on v0

v1 whole, which is shorter than its diff:
```python
import jax
import jax.numpy as jnp
from jax import lax
from jax.experimental import pallas as pl
from jax.experimental.pallas import tpu as pltpu
from jax.sharding import PartitionSpec as P

F32 = jnp.float32
BF = jnp.bfloat16
N = 16
LN2 = 0.6931471805599453
MASKED = -300.0
EPS = 1e-06


def nn(a, b):
    return lax.dot_general(a, b, (((1,), (0,)), ((), ())), preferred_element_type=F32)


def nt(a, b):
    return lax.dot_general(a, b, (((1,), (1,)), ((), ())), preferred_element_type=F32)


def iota(shape, dim):
    return lax.broadcasted_iota(jnp.int32, shape, dim)


def block_of(i, size=128):
    return pl.ds(pl.multiple_of(i * size, size), size)


def peer(axis, k):
    return lax.rem(lax.axis_index(axis) + k + N, N)


def greet(axes):
    barrier = pltpu.get_barrier_semaphore()

    def signal(k, _):
        for axis in axes:
            pl.semaphore_signal(
                barrier, inc=1, device_id={axis: peer(axis, k)}, device_id_type=pl.DeviceIdType.MESH
            )
        return 0

    lax.fori_loop(1, N, signal, 0)
    return lambda: pl.semaphore_wait(barrier, (N - 1) * len(axes))


def remote(src, dst, send, recv, axis, where):
    return pltpu.make_async_remote_copy(
        src_ref=src,
        dst_ref=dst,
        send_sem=send,
        recv_sem=recv,
        device_id={axis: where},
        device_id_type=pl.DeviceIdType.MESH,
    )


def to_all(make):
    def start(k, _):
        make(k).start()
        return 0

    def wait(k, _):
        make(k).wait()
        return 0

    lax.fori_loop(1, N, start, 0)
    return lambda: lax.fori_loop(1, N, wait, 0)


def split(x):
    high = x.astype(BF)
    return high, (x - high.astype(F32)).astype(BF)


def front(
    feat, wconv, tab, noise, embed, proj, cot,
    noisy, tokens, incoming, ew_kv, ew_q, slots,
    actf, actp, conv, edge_out, edge_in, gath,
    edge_send, edge_recv, dp_send, dp_recv, seq_send, seq_recv, cot_send, cot_recv, own_sem,
):
    slab = lax.axis_index("dp")
    row = lax.axis_index("seq")
    entered = greet(("dp", "seq"))

    for q in range(4):
        x = feat[:, q * 128 : q * 128 + 128].astype(F32)
        actf[q] = x / (1.0 + jnp.exp(-x))
    entered()

    own = pltpu.make_async_copy(cot.at[:, block_of(row)], incoming.at[block_of(row)], own_sem)
    own.start()
    cot_wait = to_all(
        lambda k: remote(
            cot.at[:, block_of(peer("seq", k))], incoming.at[block_of(row)],
            cot_send.at[k], cot_recv.at[k], "seq", peer("seq", k),
        )
    )

    for part in range(4):
        r, b = part // 2, part % 2
        for t in range(8):
            for q in range(4):
                rows = actf[q, pl.ds(t * 64 + r * 32 + b, 16, stride=2), :]
                actp[pl.ds((part * 8 + t) * 16, 16), q * 128 : q * 128 + 128] = rows.astype(BF)
    conv[...] = nt(wconv[...], actp[...])

    by_clip = tab[...].T
    frames, group, offset, times = [by_clip[0:32, i : i + 1] for i in range(4)]
    earlier = iota((32, 128), 1) < iota((32, 128), 0)
    starts = jnp.sum(jnp.where(earlier, tab[0:1, :], 0.0), axis=1, keepdims=True)
    lane = iota((1, 128), 1)
    slot_i = lax.shift_right_logical(lane, 4)
    col_i = lax.bitwise_and(lane, 15)
    slot = slot_i.astype(F32)
    in_slot = (group == slab.astype(F32)) & (slot >= offset) & (slot < offset + frames)
    over_clips = lambda v: jnp.sum(jnp.where(in_slot, v, 0.0), axis=0, keepdims=True)
    number = iota((32, 128), 0).astype(F32)
    usable = over_clips(1.0 + 0.0 * number)
    usable = jnp.where(usable > 0.0, 1.0, 0.0)
    segment = over_clips(number + 1.0) - 1.0
    source = over_clips(starts + slot - offset)
    level = over_clips(times + 0.0 * number)
    slots[0:1, :] = segment
    slots[1:2, :] = usable
    slots[2:8, :] = jnp.zeros((6, 128), F32)

    def own_start(frame):
        inside = (starts <= frame) & (frame < starts + frames)
        return jnp.sum(jnp.where(inside, starts, 0.0), axis=0, keepdims=True)

    here = slab.astype(F32) * 8.0 + slot
    after = here + 8.0
    start_here, start_after = own_start(here), own_start(after)
    keep = []
    for dt in range(3):
        main = (here - dt >= start_here) & (slot_i >= dt)
        late = (after - dt >= start_after) & (slot_i < dt)
        keep.append((jnp.where(main, 1.0, 0.0), jnp.where(late, 1.0, 0.0)))

    not_first = jnp.where(col_i > 0, 1.0, 0.0)
    not_last = jnp.where(col_i < 15, 1.0, 0.0)

    def tap(dt, dr, dw, r, ob):
        at = (((2 - dt) * 3 + dr + 1) * 3 + dw + 1) * 16
        b = (ob + dw) % 2
        piece = conv[at : at + 16, (r * 2 + b) * 128 : (r * 2 + b) * 128 + 128]
        if ob + dw == -1:
            return pltpu.roll(piece, 1, 1) * not_first
        if ob + dw == 2:
            return pltpu.roll(piece, 127, 1) * not_last
        return piece

    mains, lates = {}, {}
    for out_row in range(-1, 3):
        for ob in range(2):
            main = late = None
            for dt in range(3):
                total = None
                for r in range(2):
                    dr = r - out_row
                    if abs(dr) <= 1:
                        for dw in range(-1, 2):
                            term = tap(dt, dr, dw, r, ob)
                            total = term if total is None else total + term
                if dt:
                    total = pltpu.roll(total, 16 * dt, 1)
                m = total * keep[dt][0]
                main = m if main is None else main + m
                if dt:
                    m = total * keep[dt][1]
                    late = m if late is None else late + m
            mains[out_row, ob], lates[out_row, ob] = main, late
    for side, out_row in ((0, -1), (1, 2)):
        for ob in range(2):
            edge_out[side, ob * 16 : ob * 16 + 16, :] = mains[out_row, ob]
            edge_out[side, 32 + ob * 16 : 48 + ob * 16, :] = lates[out_row, ob]

    up = remote(edge_out.at[0], edge_in.at[1], edge_send.at[0], edge_recv.at[1], "seq", peer("seq", -1))
    down = remote(edge_out.at[1], edge_in.at[0], edge_send.at[1], edge_recv.at[0], "seq", peer("seq", 1))

    @pl.when(row > 0)
    def _():
        up.start()

    @pl.when(row < N - 1)
    def _():
        down.start()

    @pl.when(row == 0)
    def _():
        edge_in[0] = jnp.zeros((64, 128), F32)

    @pl.when(row == N - 1)
    def _():
        edge_in[1] = jnp.zeros((64, 128), F32)

    for j in range(3):
        high, low = split(nn(embed[...], proj[j]))
        if j == 0:
            both = jnp.concatenate([high.astype(F32), low.astype(F32)], axis=0)
            ew_q[...] = both.T.astype(BF)
        else:
            ew_kv[0:64, (j - 1) * 128 : j * 128] = high
            ew_kv[64:128, (j - 1) * 128 : j * 128] = low

    @pl.when(row > 0)
    def _():
        up.wait_send()
        down.wait_recv()

    @pl.when(row < N - 1)
    def _():
        down.wait_send()
        up.wait_recv()

    packed = jnp.zeros((16, 128), F32)
    for a in range(2):
        for ob in range(2):
            ab = a * 2 + ob
            main = mains[a, ob] + edge_in[a, ob * 16 : ob * 16 + 16, :]
            late = lates[a, ob] + edge_in[a, 32 + ob * 16 : 48 + ob * 16, :]
            gath[ab * 16 : ab * 16 + 16, block_of(slab)] = main.astype(BF)
            packed = packed + (pltpu.roll(late, 32 * ab, 1) if ab else late)
    gath[64:80, block_of(slab)] = packed.astype(BF)
    mine = gath.at[:, block_of(slab)]
    gath_wait = to_all(
        lambda k: remote(mine, mine, dp_send.at[k], dp_recv.at[k], "dp", peer("dp", k))
    )

    base = source * 16.0 + col_i.astype(F32)
    k_i = iota((2048, 128), 0)
    select = jnp.where(k_i.astype(F32) == base, 1.0, 0.0).astype(BF)
    slab_of = jnp.floor(source * 0.125)
    inner = source - slab_of * 8.0
    crosses = (inner < 2.0) & (slab_of >= 1.0)
    late_at = jnp.where(crosses, (slab_of - 1.0) * 32.0 + inner * 16.0 + col_i.astype(F32), -1.0)
    k_late = lax.shift_right_logical(k_i, 7) * 32 + lax.bitwise_and(k_i, 31)
    select_late = jnp.where(k_late.astype(F32) == late_at, 1.0, 0.0).astype(BF)
    gath_wait()

    wide = lax.bitwise_and(lax.shift_right_logical(iota((16, 2048), 1), 5), 3)
    lates_all = gath[64:80, :].astype(F32)
    spread = jnp.concatenate([jnp.where(wide == ab, lates_all, 0.0) for ab in range(4)], axis=0)
    picked = nn(gath[0:64, :], select) + nn(spread.astype(BF), select_late)
    made = usable * ((1.0 - level) * picked + level * noise[...].astype(F32))
    noisy[...] = made
    tokens[:, block_of(row)] = made.astype(BF)
    tile = tokens.at[:, block_of(row)]
    token_wait = to_all(
        lambda k: remote(tile, tile, seq_send.at[k], seq_recv.at[k], "seq", peer("seq", k))
    )
    token_wait()
    cot_wait()
    own.wait()


def attention(
    tokens, ew_kv, ew_q, incoming, slots, gains, embed,
    att, proj_out, norm_out,
    two, keys, vals, keys_t, vals_t, xk, dk, dv, exps, qx, gx, dxq, dkv, nq, outs,
    parts, landed, sums, norms,
    att_send, att_recv, own_sem, rs_send, rs_recv, nrm_send, nrm_recv, ag_send, ag_recv,
):
    slab = lax.axis_index("dp")
    head = lax.axis_index("seq")
    entered = greet(("dp", "seq"))
    scale = 128.0**-0.5
    gain_k = gains[1:2, :]
    gain_q = gains[...].T[:, 0:1]
    seg_row, use_row = slots[0:1, :], slots[1:2, :]
    seg_col = slots[...].T[:, 0:1]
    class_l = iota((128, 128), 1).astype(F32) - 1.0
    class_s = iota((128, 128), 0).astype(F32) - 1.0
    key_mask = jnp.where(class_l == seg_col, 0.0, MASKED).astype(BF)
    query_mask = jnp.where(class_s == seg_row, 1.0, 0.0).astype(BF)
    ones_two = jnp.where(iota((256, 128), 1) < 2, 1.0, 0.0).astype(BF)
    use_q = jnp.concatenate([use_row, use_row], axis=1)

    qx[128:256, 0:128] = query_mask
    qx[128:256, 128:256] = query_mask
    gx[128:256, :] = jnp.zeros((128, 256), BF)
    vals_t[128:144, :] = jnp.ones((16, 2048), BF)
    dk[...] = jnp.zeros((2048, 128), F32)
    dv[...] = jnp.zeros((2048, 128), F32)
    nq[...] = jnp.zeros((128, 256), F32)

    def prepare(i, _):
        at = block_of(i, 256)
        piece = tokens[:, at].astype(F32)
        tile = jnp.concatenate([piece, piece], axis=0).T.astype(BF)
        two[at, :] = tile
        kv = nn(tile, ew_kv[...])
        x = kv[:, 0:128]
        xk[at, :] = x
        r = lax.rsqrt(jnp.mean(x * x, axis=1, keepdims=True) + EPS)
        key = x * r * gain_k
        keys[at, 0:128] = key.astype(BF)
        keys[at, 128:256] = jnp.concatenate([key_mask, key_mask], axis=0)
        keys_t[:, at] = key.T.astype(BF)
        val = kv[:, 128:256]
        vals[at, 0:128] = val.astype(BF)
        vals[at, 128:256] = ones_two
        vals_t[0:128, at] = val.T.astype(BF)
        return 0

    lax.fori_loop(0, 8, prepare, 0)
    entered()

    def send_out(p):
        return remote(
            outs.at[block_of(p)], att.at[:, block_of(head)], att_send.at[p], att_recv.at[head], "seq", p
        )

    def own_out():
        return pltpu.make_async_copy(outs.at[block_of(head)], att.at[:, block_of(head)], own_sem)

    def query_block(i, _):
        qb = lax.rem(lax.div(head, 2) + i, 8)
        at = block_of(qb, 256)
        tile = two[at, :]
        x = nt(ew_q[...], tile)
        r = lax.rsqrt(jnp.mean(x * x, axis=0, keepdims=True) + EPS)
        query = (x * (r * (scale / LN2)) * gain_q).astype(BF)
        qx[0:128, :] = query
        out = jnp.zeros((144, 256), F32)
        for c in range(4):
            kc = pl.ds(c * 512, 512)
            e = jnp.exp2(nn(keys[kc, :], qx[...])).astype(BF)
            exps[kc, :] = e
            out = out + nn(vals_t[:, kc], e)
        inverse = 1.0 / out[128:129, :]
        out = out[0:128, :] * inverse
        outs[at, :] = (out * use_q).T.astype(BF)
        for p in (qb * 2, qb * 2 + 1):
            @pl.when(p != head)
            def _():
                send_out(p).start()

            @pl.when(p == head)
            def _():
                own_out().start()

        up = jnp.where(use_q > 0.0, incoming[at, :].astype(F32).T, 0.0)
        up = (up * inverse).astype(BF)
        delta = jnp.sum(up.astype(F32) * out, axis=0, keepdims=True)
        high, low = split(-delta)
        line = iota((16, 256), 0)
        extra = jnp.where(line == 0, high.astype(F32), jnp.where(line == 1, low.astype(F32), 0.0))
        gx[0:128, :] = up
        gx[128:144, :] = extra.astype(BF)
        dq = jnp.zeros((128, 256), F32)
        for c in range(4):
            kc = pl.ds(c * 512, 512)
            e = exps[kc, :]
            ds = (e.astype(F32) * nn(vals[kc, :], gx[...])).astype(BF)
            dv[kc, :] = dv[kc, :] + nt(e, up)
            dk[kc, :] = dk[kc, :] + nt(ds, query)
            dq = dq + nn(keys_t[:, kc], ds)
        dq = dq * scale
        nq[...] = nq[...] + dq * x * r
        scaled = gain_q * dq
        mean = jnp.mean(x * scaled, axis=0, keepdims=True)
        dxq[:, at] = (r * scaled - x * (r * r * r * mean)).astype(BF)
        return 0

    lax.fori_loop(0, 8, query_block, 0)

    def key_back(i, total):
        at = block_of(i, 256)
        x = xk[at, :]
        r = lax.rsqrt(jnp.mean(x * x, axis=1, keepdims=True) + EPS)
        grad = dk[at, :] * LN2
        scaled = gain_k * grad
        mean = jnp.mean(x * scaled, axis=1, keepdims=True)
        dkv[at, 0:128] = (r * scaled - x * (r * r * r * mean)).astype(BF)
        dkv[at, 128:256] = dv[at, :].astype(BF)
        return total + jnp.sum(grad * x * r, axis=0, keepdims=True)

    norm_k = lax.fori_loop(0, 8, key_back, jnp.zeros((1, 128), F32))
    norm_q = jnp.sum(nq[...], axis=1, keepdims=True)
    norm_q = jnp.broadcast_to(norm_q, (128, 128)).T[0:1, :]
    line = iota((8, 128), 0)
    norms[head] = jnp.where(line == 0, norm_q, jnp.where(line == 1, norm_k, 0.0))
    norm_wait = to_all(
        lambda k: remote(
            norms.at[head], norms.at[head], nrm_send.at[k], nrm_recv.at[k], "seq", peer("seq", k)
        )
    )
    part_q = nn(dxq[...], two[...]).T
    part_kv = nn(tokens[...], dkv[...])
    for b in range(8):
        rows = slice(b * 8, b * 8 + 8)
        parts[2 * b, :, 0:128] = part_q[rows, :]
        parts[2 * b, :, 128:256] = part_kv[rows, 0:128]
        parts[2 * b + 1, :, 0:128] = part_kv[rows, 128:256]
        parts[2 * b + 1, :, 128:256] = jnp.zeros((8, 128), F32)
    landed[slab] = parts[slab]
    rs_wait = to_all(
        lambda k: remote(
            parts.at[peer("dp", k)], landed.at[slab], rs_send.at[k], rs_recv.at[k], "dp", peer("dp", k)
        )
    )
    columns = embed[:, block_of(slab)].astype(F32).T.astype(BF)
    norm_wait()
    rs_wait()
    total, norm = landed[0], norms[0]
    for j in range(1, N):
        total, norm = total + landed[j], norm + norms[j]
    sums[slab, 0:8, :] = total
    sums[slab, 8:16, 0:128] = norm
    sums[slab, 8:16, 128:256] = jnp.zeros((8, 128), F32)
    ag_wait = to_all(
        lambda k: remote(
            sums.at[slab], sums.at[slab], ag_send.at[k], ag_recv.at[k], "dp", peer("dp", k)
        )
    )
    ag_wait()
    even = jnp.concatenate([sums[2 * b, 0:8, :] for b in range(8)], axis=0)
    odd = jnp.concatenate([sums[2 * b + 1, 0:8, 0:128] for b in range(8)], axis=0)
    norm = sums[0, 8:16, 0:128]
    for j in range(1, N):
        norm = norm + sums[j, 8:16, 0:128]
    norm_out[...] = norm
    whole = jnp.concatenate([even, odd], axis=1)
    high, low = split(whole)
    grads = nn(columns, high) + nn(columns, low)
    for j in range(3):
        proj_out[pl.ds(j, 128, stride=3), :] = grads[:, j * 128 : j * 128 + 128]

    def out_wait(p, _):
        @pl.when(p != head)
        def _():
            send_out(p).wait_send()
            remote(
                outs.at[block_of(p)], att.at[:, block_of(p)], att_send.at[p], att_recv.at[p], "seq", p
            ).wait_recv()

        return 0

    lax.fori_loop(0, N, out_wait, 0)
    own_out().wait()


def body(
    features,
    conv_weight,
    clip_frames,
    clip_group,
    clip_offset,
    clip_times,
    noise_tokens,
    embed_weight,
    attention_proj,
    norm_gains,
    cotangent,
):
    vmem = pl.BlockSpec(memory_space=pltpu.VMEM)
    tab = jnp.stack([clip_frames.astype(F32), clip_group.astype(F32), clip_offset.astype(F32), clip_times])
    tab = jnp.pad(tab, ((0, 4), (0, 96)))
    dma = pltpu.SemaphoreType.DMA
    shape = jax.ShapeDtypeStruct
    noisy, tokens, incoming, ew_kv, ew_q, slots = pl.pallas_call(
        front,
        name="front",
        out_shape=(
            shape((64, 128), F32),
            shape((64, 2048), BF),
            shape((2048, 128), BF),
            shape((128, 256), BF),
            shape((128, 128), BF),
            shape((8, 128), F32),
        ),
        in_specs=[vmem] * 7,
        out_specs=[vmem] * 6,
        scratch_shapes=[
            pltpu.VMEM((4, 512, 128), F32),
            pltpu.VMEM((512, 512), BF),
            pltpu.VMEM((432, 512), F32),
            pltpu.VMEM((2, 64, 128), F32),
            pltpu.VMEM((2, 64, 128), F32),
            pltpu.VMEM((80, 2048), BF),
            dma((2,)),
            dma((2,)),
            dma((N,)),
            dma((N,)),
            dma((N,)),
            dma((N,)),
            dma((N,)),
            dma((N,)),
            dma,
        ],
        compiler_params=pltpu.CompilerParams(
            collective_id=0, has_side_effects=True, vmem_limit_bytes=40 * 2**20
        ),
    )(
        features.reshape(512, 512),
        conv_weight.reshape(432, 512),
        tab,
        noise_tokens.transpose(0, 2, 1).reshape(64, 128),
        embed_weight,
        attention_proj.transpose(1, 2, 0, 3).reshape(3, 2048, 128),
        cotangent.reshape(128, 2048),
    )
    att, grads, norms = pl.pallas_call(
        attention,
        name="attention",
        out_shape=(shape((128, 2048), BF), shape((384, 128), F32), shape((8, 128), F32)),
        in_specs=[vmem] * 7,
        out_specs=[vmem] * 3,
        scratch_shapes=[
            pltpu.VMEM((2048, 128), BF),
            pltpu.VMEM((2048, 256), BF),
            pltpu.VMEM((2048, 256), BF),
            pltpu.VMEM((128, 2048), BF),
            pltpu.VMEM((144, 2048), BF),
            pltpu.VMEM((2048, 128), F32),
            pltpu.VMEM((2048, 128), F32),
            pltpu.VMEM((2048, 128), F32),
            pltpu.VMEM((2048, 256), BF),
            pltpu.VMEM((256, 256), BF),
            pltpu.VMEM((256, 256), BF),
            pltpu.VMEM((128, 2048), BF),
            pltpu.VMEM((2048, 256), BF),
            pltpu.VMEM((128, 256), F32),
            pltpu.VMEM((2048, 128), BF),
            pltpu.VMEM((N, 8, 256), F32),
            pltpu.VMEM((N, 8, 256), F32),
            pltpu.VMEM((N, 16, 256), F32),
            pltpu.VMEM((N, 8, 128), F32),
            dma((N,)),
            dma((N,)),
            dma,
            dma((N,)),
            dma((N,)),
            dma((N,)),
            dma((N,)),
            dma((N,)),
            dma((N,)),
        ],
        compiler_params=pltpu.CompilerParams(
            collective_id=1, has_side_effects=True, vmem_limit_bytes=48 * 2**20
        ),
    )(tokens, ew_kv, ew_q, incoming, slots, norm_gains, embed_weight)
    return (
        noisy.reshape(1, 64, 128).transpose(0, 2, 1),
        att.reshape(1, 128, 2048),
        grads.reshape(128, 3, 1, 128),
        norms[0:2],
    )


def solution(mesh):
    return jax.shard_map(
        body,
        mesh=mesh,
        in_specs=(
            P("dp", "seq", None, None),
            P(),
            P(),
            P(),
            P(),
            P(),
            P("dp", "seq", None),
            P(),
            P(None, None, "seq", None),
            P(),
            P("dp", "seq", None),
        ),
        out_specs=(P("dp", "seq", None), P("dp", "seq", None), P("dp", None, "seq", None), P()),
        check_vma=False,
    )
```

time: 382 us -> 88.4 us (0.23)
  waiting for transfers between devices: 136 us -> 0 us
  matrix products: 79.2 us -> 0 us
  Pallas kernels: 0 us -> 76.4 us
  blocking collectives: 75.7 us -> 0 us
  starting transfers between devices: 24.7 us -> 0 us
  other arithmetic: 23 us -> 2 us
  local copies, waits for them, and re-layouts: 27.2 us -> 8.82 us
  between operations: 14.3 us -> 0.68 us
    dot_general x55 -> x0, matrix products: 79.2 us -> none  [the longest x4 11 us: block_step(): jnp.einsum('hbs,bhe->she', probs_bf, grad_blk, preferred_element_type=jnp...]
    unnamed x4 -> x0, waiting for transfers between devices: 77.8 us -> none
    pallas_call x0 -> x2, Pallas kernels: none -> 76.4 us  [the longest x1 39.6 us: body(): pl.pallas_call(front, name='front', out_shape=(shape((64, 128), F32), sha...]
    psum x1 -> x0, blocking collectives: 75.7 us -> none  [body(): norm_grad = lax.psum(jnp.stack([query_gain, key_gain]), ('dp', 'seq'))]
    all_gather x1 -> x0, waiting for transfers between devices: 33.4 us -> none  [body(): hidden = lax.all_gather(local_hidden, 'seq', axis=0, tiled=True)]
    all_to_all x2 -> x0, waiting for transfers between devices: 18.9 us -> none  [the longest x1 18.9 us: body(): lax.all_to_all(cot_rows, 'seq', split_axis=1, concat_axis=0, tiled=True)]
    all_to_all x2 -> x0, starting transfers between devices: 14.1 us -> none  [the longest x1 9.29 us: body(): lax.all_to_all(cot_rows, 'seq', split_axis=1, concat_axis=0, tiled=True)]
    ppermute x3 -> x0, starting transfers between devices: 10.3 us -> none  [the longest x1 4.39 us: padded_2(): before = lax.ppermute(last, axis, up)]
  transfers between devices with their start and end apart: 8 -> 0, of which waited for: 5 -> 0; matrix products, arithmetic and copies ran while one was open for 4% -> 0% of each run, Pallas kernels for 0% -> 0%
where the time goes in v1:
time: 88.4 us; the launch traced here: 87.9 us
  Pallas kernels  76.4 us (86%)
  local copies, waits for them, and re-layouts  8.82 us (10%)
  other arithmetic  2 us (2%)
    pallas_call x1, Pallas kernels, body(): pl.pallas_call(front, name='front', out_shape=(shape((64, 128), F32), sha...  39.6 us
    pallas_call x1, Pallas kernels, body(): pl.pallas_call(attention, name='attention', out_shape=(shape((128, 2048),...  36.8 us
    unnamed x19, local copies, waits for them, and re-layouts  8.25 us
    another operation x3, other arithmetic, body(): jnp.stack([clip_frames.astype(F32), clip_group.astype(F32), clip_offset.a...  2 us

profile of v1, /device:TPU:1, one launch (start us, length us, event | category | flops | bytes accessed | tf_op | source)
XLA Modules:
  0.0 87.9 jit_solution(8632788050680639433)
XLA Ops:
  0.6 0.7 convert_bitcast_fusion.2
  1.3 0.7 convert_bitcast_fusion
  2.0 0.7 select_maximum_fusion.tab
  2.6 0.0 copy-start
  2.6 1.4 %copy-done = bf16[2048,3,1,128]{3,0,2,1:T(8,128)(2,1)S(1)} copy-done((bf16[2048,3,1,128]{3,0,2,1:T(8,128)(2,1)S(1)}, bf16[2048,3,1,128]{3,0,2,1:T(8,128)(2,1)}, u32[]{:S(2)}) %copy-start) | copy-done | bytes 1572888
  4.0 0.0 copy-start.1
  4.0 0.9 %copy-done.1 = bf16[64,2048]{1,0:T(8,128)(2,1)S(1)} copy-done((bf16[64,2048]{1,0:T(8,128)(2,1)S(1)}, bf16[64,2048]{1,0:T(8,128)(2,1)}, u32[]{:S(2)}) %copy-start.1) | copy-done | bytes 262168
  5.0 0.0 copy-start.3
  5.0 1.0 %copy-done.3 = bf16[8,2,32,512]{3,2,1,0:T(8,128)(2,1)S(1)} copy-done((bf16[8,2,32,512]{3,2,1,0:T(8,128)(2,1)S(1)}, bf16[8,2,32,512]{3,2,1,0:T(8,128)(2,1)}, u32[]{:S(2)}) %copy-start.3) | copy-done | bytes 524312
  6.0 0.0 copy-start.4
  6.0 1.0 %copy-done.4 = bf16[1,128,2048]{2,1,0:T(8,128)(2,1)S(1)} copy-done((bf16[1,128,2048]{2,1,0:T(8,128)(2,1)S(1)}, bf16[1,128,2048]{2,1,0:T(8,128)(2,1)}, u32[]{:S(2)}) %copy-start.4) | copy-done | bytes 524312
  7.1 0.0 copy-start.5
  7.1 1.0 %copy-done.5 = bf16[3,3,3,16,512]{4,3,2,1,0:T(8,128)(2,1)S(1)} copy-done((bf16[3,3,3,16,512]{4,3,2,1,0:T(8,128)(2,1)S(1)}, bf16[3,3,3,16,512]{4,3,2,1,0:T(8,128)(2,1)}, u32[]{:S(2)}) %copy-start.5) | copy-done | bytes 442392
  8.1 0.0 copy-start.6
  8.1 0.7 copy-done.6
  8.8 0.0 copy-start.2
  8.8 0.0 copy-start.7
  8.8 39.6 %front.1 = (f32[64,128]{1,0:T(8,128)S(1)}, bf16[64,2048]{1,0:T(8,128)(2,1)S(1)}, bf16[2048,128]{1,0:T(8,128)(2,1)S(1)}, bf16[128,256]{1,0:T(8,128)(2,1)S(1)}, bf...) custom-call(bf16[512,512]{1,0:T(8,128)(2,1)S(1)} %bitcast.24, bf16[432,512]{1,0:T(8,128)(2,1)S(1)} %bitcast.27, ...), custom_call_target="tpu_custom_call" | custom-call | tf_op jit(solution)/shard_map/front/pallas_call | solution.py:466
  48.4 0.0 copy-done.2
  48.4 0.0 copy-done.7
  48.4 36.8 %attention.1 = (bf16[128,2048]{1,0:T(8,128)(2,1)S(1)}, f32[384,128]{1,0:T(8,128)S(1)}, f32[8,128]{1,0:T(8,128)S(1)}) custom-call(bf16[64,2048]{1,0:T(8,128)(2,1)S(1)} %get-tuple-element.14.tokens, bf16[128,256]{1,0:T(8,128)(2,1)S(1)} %get-tuple-element.15.ew_kv, bf16[128,128]{1,0:T(8,128)(2,1)S(1)} %get-tuple-element.16.ew_q, ...), custom_call_target="tpu_custom_call" | custom-call | tf_op jit(solution)/shard_map/attention/pallas_call | solution.py:508
  85.2 0.6 slice.3
  85.8 0.6 copy.22
  86.4 0.8 copy.23
  87.2 0.7 copy.24
Async XLA Ops:
  2.6 1.4 %copy-start = (bf16[2048,3,1,128]{3,0,2,1:T(8,128)(2,1)S(1)}, bf16[2048,3,1,128]{3,0,2,1:T(8,128)(2,1)}, u32[]{:S(2)}) copy-start(bf16[2048,3,1,128]{3,0,2,1:T(8,128)(2,1)} %param.19) | copy-start | bytes 4718596
  4.0 0.9 %copy-start.1 = (bf16[64,2048]{1,0:T(8,128)(2,1)S(1)}, bf16[64,2048]{1,0:T(8,128)(2,1)}, u32[]{:S(2)}) copy-start(bf16[64,2048]{1,0:T(8,128)(2,1)} %embed.3) | copy-start | bytes 786436
  5.0 1.0 %copy-start.3 = (bf16[8,2,32,512]{3,2,1,0:T(8,128)(2,1)S(1)}, bf16[8,2,32,512]{3,2,1,0:T(8,128)(2,1)}, u32[]{:S(2)}) copy-start(bf16[8,2,32,512]{3,2,1,0:T(8,128)(2,1)} %param.11) | copy-start | bytes 1572868
  6.0 1.0 %copy-start.4 = (bf16[1,128,2048]{2,1,0:T(8,128)(2,1)S(1)}, bf16[1,128,2048]{2,1,0:T(8,128)(2,1)}, u32[]{:S(2)}) copy-start(bf16[1,128,2048]{2,1,0:T(8,128)(2,1)} %param.21) | copy-start | bytes 1572868
  7.1 1.0 %copy-start.5 = (bf16[3,3,3,16,512]{4,3,2,1,0:T(8,128)(2,1)S(1)}, bf16[3,3,3,16,512]{4,3,2,1,0:T(8,128)(2,1)}, u32[]{:S(2)}) copy-start(bf16[3,3,3,16,512]{4,3,2,1,0:T(8,128)(2,1)} %param.12) | copy-start | bytes 1327108
  8.1 0.7 copy-start.6
  8.8 39.6 %copy-start.2 = (bf16[64,2048]{1,0:T(8,128)(2,1)S(1)}, bf16[64,2048]{1,0:T(8,128)(2,1)}, u32[]{:S(2)}) copy-start(bf16[64,2048]{1,0:T(8,128)(2,1)} %embed.3) | copy-start | bytes 786436
  8.8 39.6 %copy-start.7 = (f32[2,128]{1,0:T(2,128)S(1)}, f32[2,128]{1,0:T(2,128)}, u32[]{:S(2)}) copy-start(f32[2,128]{1,0:T(2,128)} %gains.1) | copy-start | bytes 3076

commit v2 on v1

v2 whole, which is shorter than its diff:
```python
import jax
import jax.numpy as jnp
from jax import lax
from jax.experimental import pallas as pl
from jax.experimental.pallas import tpu as pltpu
from jax.sharding import PartitionSpec as P

F32 = jnp.float32
BF = jnp.bfloat16
N = 16
LN2 = 0.6931471805599453
MASKED = -300.0
EPS = 1e-06


def nn(a, b):
    return lax.dot_general(a, b, (((1,), (0,)), ((), ())), preferred_element_type=F32)


def nt(a, b):
    return lax.dot_general(a, b, (((1,), (1,)), ((), ())), preferred_element_type=F32)


def iota(shape, dim):
    return lax.broadcasted_iota(jnp.int32, shape, dim)


def block_of(i, size=128):
    return pl.ds(pl.multiple_of(i * size, size), size)


def peer(axis, k):
    return lax.rem(lax.axis_index(axis) + k + N, N)


def greet():
    barrier = pltpu.get_barrier_semaphore()

    def signal(**where):
        pl.semaphore_signal(barrier, inc=1, device_id=where, device_id_type=pl.DeviceIdType.MESH)

    def both(k, _):
        signal(dp=peer("dp", k))
        signal(seq=peer("seq", k))
        return 0

    lax.fori_loop(1, N, both, 0)
    for a in (-1, 1):
        for b in (-1, 1):
            signal(dp=peer("dp", a), seq=peer("seq", b))
    return lambda: pl.semaphore_wait(barrier, 2 * (N - 1) + 4)


def remote(src, dst, send, recv, **where):
    return pltpu.make_async_remote_copy(
        src_ref=src,
        dst_ref=dst,
        send_sem=send,
        recv_sem=recv,
        device_id=where,
        device_id_type=pl.DeviceIdType.MESH,
    )


def to_all(make):
    def start(k, _):
        make(k).start()
        return 0

    def wait(k, _):
        make(k).wait()
        return 0

    lax.fori_loop(1, N, start, 0)
    return lambda: lax.fori_loop(1, N, wait, 0)


def split(x):
    high = x.astype(BF)
    return high, (x - high.astype(F32)).astype(BF)


def whole(
    feat_h, wconv_h, frames_h, group_h, offset_h, times_h, noise_h, embed_h, proj_h, gains_h, cot,
    noisy, att, proj_out, norm_out,
    feat, wconv, ints, times_v, noise, embed, proj, gains,
    tab, actf, actp, conv, edge_out, late_out, own_late, edge_in, late_in, own_late_in, gath,
    tokens, incoming, ew, keys, vals, keys_t, vals_t, xq, xk, rq, rk, qx, gx, q_n, up_n, out_t, inv, even, odd, dss, dxq, dkv, outs,
    parts_kv, parts_q, landed_kv, sums, norms,
    in_sem, edge_send, edge_recv, dp_send, dp_recv, z_send, z_recv, sib_send, sib_recv,
    cot_send, cot_recv, own_sem, att_send, att_recv, kv_send, kv_recv, q_send, q_recv,
    nrm_send, nrm_recv, ag_send, ag_recv,
):
    slab = lax.axis_index("dp")
    row = lax.axis_index("seq")
    other = row + 1 - 2 * lax.rem(row, 2)
    fetches = []
    for src, dst in (
        (feat_h, feat), (wconv_h, wconv), (frames_h, ints.at[0]), (group_h, ints.at[1]), (offset_h, ints.at[2]),
        (times_h, times_v), (embed_h, embed), (proj_h, proj), (noise_h, noise), (gains_h, gains),
    ):
        fetches.append(pltpu.make_async_copy(src, dst, in_sem.at[len(fetches)]))
        fetches[-1].start()
    entered = greet()
    fetches[0].wait()
    for q in range(4):
        x = feat[:, q * 128 : q * 128 + 128].astype(F32)
        actf[q] = x / (1.0 + jnp.exp(-x))

    for part in range(4):
        r, b = part // 2, part % 2
        for t in range(8):
            for q in range(4):
                rows = actf[q, pl.ds(t * 64 + r * 32 + b, 16, stride=2), :]
                actp[pl.ds((part * 8 + t) * 16, 16), q * 128 : q * 128 + 128] = rows.astype(BF)
    fetches[1].wait()
    conv[...] = nt(wconv[...], actp[...])

    for i in range(2, 6):
        fetches[i].wait()
    tab[...] = jnp.zeros((8, 128), F32)
    for i in range(3):
        tab[i : i + 1, 0:32] = ints[i].astype(F32)
    tab[3:4, 0:32] = times_v[...]
    by_clip = tab[...].T
    frames, group, offset, times = [by_clip[0:32, i : i + 1] for i in range(4)]
    earlier = iota((32, 128), 1) < iota((32, 128), 0)
    starts = jnp.sum(jnp.where(earlier, tab[0:1, :], 0.0), axis=1, keepdims=True)
    lane = iota((1, 128), 1)
    slot_i = lax.shift_right_logical(lane, 4)
    col_i = lax.bitwise_and(lane, 15)
    slot = slot_i.astype(F32)
    in_slot = (group == slab.astype(F32)) & (slot >= offset) & (slot < offset + frames)
    over_clips = lambda v: jnp.sum(jnp.where(in_slot, v, 0.0), axis=0, keepdims=True)
    number = iota((32, 128), 0).astype(F32)
    usable = over_clips(1.0 + 0.0 * number)
    usable = jnp.where(usable > 0.0, 1.0, 0.0)
    segment = over_clips(number + 1.0) - 1.0
    source = over_clips(starts + slot - offset)
    level = over_clips(times + 0.0 * number)

    def own_start(frame):
        inside = (starts <= frame) & (frame < starts + frames)
        return jnp.sum(jnp.where(inside, starts, 0.0), axis=0, keepdims=True)

    here = slab.astype(F32) * 8.0 + slot
    after = here + 8.0
    start_here, start_after = own_start(here), own_start(after)
    keep = []
    for dt in range(3):
        main = (here - dt >= start_here) & (slot_i >= dt)
        late = (after - dt >= start_after) & (slot_i < dt)
        keep.append((jnp.where(main, 1.0, 0.0), jnp.where(late, 1.0, 0.0)))

    not_first = jnp.where(col_i > 0, 1.0, 0.0)
    not_last = jnp.where(col_i < 15, 1.0, 0.0)

    def tap(dt, dr, dw, r, ob):
        at = (((2 - dt) * 3 + dr + 1) * 3 + dw + 1) * 16
        b = (ob + dw) % 2
        piece = conv[at : at + 16, (r * 2 + b) * 128 : (r * 2 + b) * 128 + 128]
        if ob + dw == -1:
            return pltpu.roll(piece, 1, 1) * not_first
        if ob + dw == 2:
            return pltpu.roll(piece, 127, 1) * not_last
        return piece

    def sums_of(out_row, ob):
        main = late = None
        for dt in range(3):
            total = None
            for r in range(2):
                dr = r - out_row
                if abs(dr) <= 1:
                    for dw in range(-1, 2):
                        term = tap(dt, dr, dw, r, ob)
                        total = term if total is None else total + term
            if dt:
                total = pltpu.roll(total, 16 * dt, 1)
            m = total * keep[dt][0]
            main = m if main is None else main + m
            if dt:
                m = total * keep[dt][1]
                late = m if late is None else late + m
        return main, late

    for side, out_row in ((0, -1), (1, 2)):
        for ob in range(2):
            at = slice(ob * 16, ob * 16 + 16)
            edge_out[side, at, :], late_out[side, at, :] = sums_of(out_row, ob)
    mains = {}
    for a in range(2):
        for ob in range(2):
            at = slice((a * 2 + ob) * 16, (a * 2 + ob) * 16 + 16)
            mains[a, ob], own_late[at, :] = sums_of(a, ob)
    entered()

    routes = []
    for side, step in ((0, -1), (1, 1)):
        goes = (row > 0) if side == 0 else (row < N - 1)
        comes = (row < N - 1) if side == 0 else (row > 0)
        routes.append((
            remote(edge_out.at[side], edge_in.at[1 - side], edge_send.at[side], edge_recv.at[side], seq=peer("seq", step)),
            goes, comes, edge_in, 1 - side,
        ))
        routes.append((
            remote(
                late_out.at[side], late_in.at[1 - side], edge_send.at[2 + side], edge_recv.at[2 + side],
                dp=peer("dp", 1), seq=peer("seq", step),
            ),
            goes & (slab < N - 1), comes & (slab > 0), late_in, 1 - side,
        ))
    routes.append((
        remote(own_late, own_late_in.at[0], edge_send.at[4], edge_recv.at[4], dp=peer("dp", 1)),
        slab < N - 1, slab > 0, own_late_in, 0,
    ))
    for copy, goes, _, _, _ in routes:
        pl.when(goes)(copy.start)
    def cot_copy(k):
        return remote(
            cot.at[:, block_of(peer("seq", k))], incoming.at[block_of(row)], cot_send.at[k], cot_recv.at[k],
            seq=peer("seq", k),
        )

    own_cot = pltpu.make_async_copy(cot.at[:, block_of(row)], incoming.at[block_of(row)], own_sem.at[0])
    own_cot.start()
    for _, _, comes, dst, i in routes:

        @pl.when(jnp.logical_not(comes))
        def _():
            dst[i] = jnp.zeros(dst.shape[1:], F32)

    fetches[6].wait()
    fetches[7].wait()
    for j in range(3):
        high, low = split(nn(embed[...], proj[j]))
        ew[0:64, j * 128 : j * 128 + 128] = high
        ew[64:128, j * 128 : j * 128 + 128] = low
    base = source * 16.0 + col_i.astype(F32)
    select = jnp.where(iota((2048, 128), 0).astype(F32) == base, 1.0, 0.0).astype(BF)
    fetches[8].wait()
    fetches[9].wait()

    for copy, goes, comes, _, _ in routes:
        pl.when(goes)(copy.wait_send)
        pl.when(comes)(copy.wait_recv)
    for a in range(2):
        for ob in range(2):
            at = slice((a * 2 + ob) * 16, (a * 2 + ob) * 16 + 16)
            side = slice(ob * 16, ob * 16 + 16)
            total = mains[a, ob] + edge_in[a, side, :] + late_in[a, side, :] + own_late_in[0, at, :]
            gath[at, block_of(slab)] = total.astype(BF)
    mine = gath.at[:, block_of(slab)]
    gath_wait = to_all(lambda k: remote(mine, mine, dp_send.at[k], dp_recv.at[k], dp=peer("dp", k)))

    for k in (1, 15, 2, 14, 3, 13):
        cot_copy(k).start()
    gath_wait()

    made = usable * ((1.0 - level) * nn(gath[...], select) + level * noise[...].astype(F32))
    noisy[...] = made
    tokens[:, block_of(row)] = made.astype(BF)

    def tile_of(k):
        return tokens.at[:, block_of(peer("seq", -2 * k))]

    def to_chip(k):
        return remote(tile_of(0), tile_of(0), z_send.at[k], z_recv.at[k], seq=peer("seq", 2 * k))

    def to_other(k):
        return remote(tile_of(k), tile_of(k), sib_send.at[k], sib_recv.at[k], seq=other)

    for k in (4, 3, 5, 2, 6, 1, 7):
        to_chip(k).start()
    to_other(0).start()
    for k in (4, 12, 5, 11, 6, 10, 7, 9, 8):
        cot_copy(k).start()

    scale = 128.0**-0.5
    gain_q, gain_k = gains[0:1, :], gains[1:2, :]
    by_lane = jnp.broadcast_to(segment, (128, 128))
    by_row = by_lane.T
    key_mask = jnp.where(iota((128, 128), 1).astype(F32) - 1.0 == by_row, 0.0, MASKED).astype(BF)
    query_mask = jnp.where(iota((128, 128), 0).astype(F32) - 1.0 == by_lane, 1.0, 0.0).astype(BF)
    ones_two = jnp.where(iota((256, 128), 1) < 2, 1.0, 0.0).astype(BF)
    use_q = jnp.concatenate([usable, usable], axis=1)
    for p in range(N):
        qx[128:256, p * 128 : p * 128 + 128] = query_mask
        keys[p * 128 : p * 128 + 128, 128:256] = key_mask
    vals_t[128:144, :] = jnp.ones((16, 2048), BF)
    gx[128:256, :] = jnp.zeros((128, 2048), BF)

    chip = lax.div(row, 2)

    def place(i):
        return block_of(lax.rem(i, 2) * 4 + lax.div(i, 2), 256)

    def prepare(chip, i):
        at, qat = block_of(chip, 256), place(i)
        piece = tokens[:, at].astype(F32)
        tile = jnp.concatenate([piece, piece], axis=0).T.astype(BF)
        qkv = nn(tile, ew[...])
        x = qkv[:, 0:128]
        xq[qat, :] = x
        r = lax.rsqrt(jnp.mean(x * x, axis=1, keepdims=True) + EPS)
        rq[qat, :] = jnp.broadcast_to(r, (256, 128))
        query = x * (r * (scale / LN2)) * gain_q
        q_n[qat, :] = query.astype(BF)
        qx[0:128, qat] = query.T.astype(BF)
        x = qkv[:, 128:256]
        xk[at, :] = x
        r = lax.rsqrt(jnp.mean(x * x, axis=1, keepdims=True) + EPS)
        rk[at, :] = jnp.broadcast_to(r, (256, 128))
        key = x * r * gain_k
        keys[at, 0:128] = key.astype(BF)
        keys_t[:, at] = key.T.astype(BF)
        val = qkv[:, 256:384]
        vals[at, 0:128] = val.astype(BF)
        vals[at, 128:256] = ones_two
        vals_t[0:128, at] = val.T.astype(BF)

    def near(i):
        half = lax.div(i, 2)
        return jnp.where(lax.rem(i, 2) == 1, half + 1, 8 - half)

    def pass_on(i):
        to_chip(near(i)).wait_recv()
        to_other(near(i)).start()

    to_other(0).wait_recv()
    prepare(chip, 0)
    pass_on(1)

    def arrive(i, _):
        pass_on(i + 1)
        to_other(near(i)).wait_recv()
        prepare(lax.rem(chip + 8 - near(i), 8), lax.rem(8 - near(i), 8))
        return 0

    lax.fori_loop(1, 7, arrive, 0)
    to_other(4).wait_recv()
    prepare(lax.rem(chip + 4, 8), 4)

    def sent(k, _):
        to_chip(k).wait_send()
        to_other(k).wait_send()
        return 0

    lax.fori_loop(1, 8, sent, 0)
    to_other(0).wait_send()

    def send_out(p):
        return remote(outs.at[block_of(p)], att.at[:, block_of(row)], att_send.at[p], att_recv.at[row], seq=p)

    own_out = pltpu.make_async_copy(outs.at[block_of(row)], att.at[:, block_of(row)], own_sem.at[1])

    def score(i, buffer, c):
        kc = pl.ds(c * 512, 512)
        buffer[kc, block_of(lax.div(i, 2), 256)] = jnp.exp2(nn(keys[kc, :], qx[:, place(i)])).astype(BF)

    def output(i, buffer, c):
        kc = pl.ds(c * 512, 512)
        return nn(vals_t[:, kc], buffer[kc, block_of(lax.div(i, 2), 256)])

    def finish(i, out):
        at = place(i)
        inverse = 1.0 / out[128:129, :]
        out = out[0:128, :] * inverse
        inv[0:1, at] = inverse
        out_t[:, at] = out
        qb = lax.rem(chip + i, 8)
        outs[block_of(qb, 256), :] = (out * use_q).T.astype(BF)
        for p in (qb * 2, qb * 2 + 1):

            @pl.when(p != row)
            def _():
                send_out(p).start()

            @pl.when(p == row)
            def _():
                own_out.start()

    def pair(i, buffer, following):
        out = jnp.zeros((144, 256), F32)
        for c in range(4):
            score(i + 1, following, c)
            out = out + output(i, buffer, c)
        finish(i, out)

    for c in range(4):
        score(0, even, c)

    def forward(j, _):
        pair(2 * j, even, odd)
        pair(2 * j + 1, odd, even)
        return 0

    lax.fori_loop(0, 3, forward, 0)
    pair(6, even, odd)
    finish(7, nn(vals_t[...], odd[:, 768:1024]))

    def cot_wait(k, _):
        cot_copy(k).wait()
        return 0

    lax.fori_loop(1, N, cot_wait, 0)
    own_cot.wait()

    def incoming_rows(i, _):
        at = place(i)
        up = jnp.where(use_q > 0.0, incoming[block_of(lax.rem(chip + i, 8), 256), :].astype(F32).T, 0.0)
        up = (up * inv[0:1, at]).astype(BF)
        wide = up.astype(F32)
        delta = jnp.sum(wide * out_t[:, at], axis=0, keepdims=True)
        high, low = split(-delta)
        line = iota((16, 256), 0)
        extra = jnp.where(line == 0, high.astype(F32), jnp.where(line == 1, low.astype(F32), 0.0))
        gx[0:128, at] = up
        gx[128:144, at] = extra.astype(BF)
        up_n[at, :] = wide.T.astype(BF)
        return 0

    lax.fori_loop(0, 8, incoming_rows, 0)

    def rms_back(x, r, gain, grad):
        scaled = gain * grad
        mean = jnp.mean(x * scaled, axis=1, keepdims=True)
        return (r * (scaled - x * (r * r * mean))).astype(BF)

    def key_block(i, total):
        at = block_of(i, 256)
        for c in range(4):
            qc = pl.ds(c * 512, 512)
            e = (even, odd)[c // 2][at, c % 2 * 512 : c % 2 * 512 + 512]
            dss[at, qc] = (e.astype(F32) * nn(vals[at, :], gx[:, qc])).astype(BF)
        dkv[at, 128:256] = (nn(even[at, :], up_n[0:1024, :]) + nn(odd[at, :], up_n[1024:2048, :])).astype(BF)
        grad = nn(dss[at, :], q_n[...]) * LN2
        x, r = xk[at, :], rk[at, :]
        dkv[at, 0:128] = rms_back(x, r, gain_k, grad)
        return total + jnp.sum(grad * x * r, axis=0, keepdims=True)

    norm_k = lax.fori_loop(0, 8, key_block, jnp.zeros((1, 128), F32))
    part = nn(tokens[...], dkv[...])
    for j in range(N):
        parts_kv[j] = part[j // 2 * 8 : j // 2 * 8 + 8, j % 2 * 128 : j % 2 * 128 + 128]
    landed_kv[slab] = parts_kv[slab]
    kv_wait = to_all(
        lambda k: remote(
            parts_kv.at[peer("dp", k)], landed_kv.at[slab], kv_send.at[k], kv_recv.at[k], dp=peer("dp", k)
        )
    )

    line = iota((8, 128), 0)
    norms[row] = jnp.where(line == 0, norm_k * gain_k / gain_q, jnp.where(line == 1, norm_k, 0.0))
    norm_wait = to_all(
        lambda k: remote(norms.at[row], norms.at[row], nrm_send.at[k], nrm_recv.at[k], seq=peer("seq", k))
    )

    def query_back(i, _):
        at = place(i)
        grad = nn(keys_t[...], dss[:, at]).T * scale
        dxq[block_of(lax.rem(chip + i, 8), 256), :] = rms_back(xq[at, :], rq[at, :], gain_q, grad)
        return 0

    lax.fori_loop(0, 8, query_back, 0)
    parts_q[slab] = nn(tokens[...], dxq[...]).astype(BF)
    q_wait = to_all(
        lambda k: remote(parts_q.at[slab], parts_q.at[slab], q_send.at[k], q_recv.at[k], dp=peer("dp", k))
    )
    columns = embed[:, block_of(slab)].astype(F32).T.astype(BF)
    kv_wait()
    norm_wait()
    for i, buffer in enumerate((landed_kv, norms)):
        total = buffer[0]
        for j in range(1, N):
            total = total + buffer[j]
        sums[slab, i * 8 : i * 8 + 8, :] = total
    ag_wait = to_all(
        lambda k: remote(sums.at[slab], sums.at[slab], ag_send.at[k], ag_recv.at[k], dp=peer("dp", k))
    )

    def out_wait(p, _):
        @pl.when(p != row)
        def _():
            send_out(p).wait_send()
            remote(outs.at[block_of(p)], att.at[:, block_of(p)], att_send.at[p], att_recv.at[p], seq=p).wait_recv()

        return 0

    lax.fori_loop(0, N, out_wait, 0)
    own_out.wait()
    q_wait()
    whole_q = parts_q[0].astype(F32)
    for j in range(1, N):
        whole_q = whole_q + parts_q[j].astype(F32)
    ag_wait()
    whole_k = jnp.concatenate([sums[2 * b, 0:8, :] for b in range(8)], axis=0)
    whole_v = jnp.concatenate([sums[2 * b + 1, 0:8, :] for b in range(8)], axis=0)
    norm = sums[0, 8:16, :]
    for j in range(1, N):
        norm = norm + sums[j, 8:16, :]
    norm_out[...] = norm[0:2, :]
    for j, part in enumerate((whole_q, whole_k, whole_v)):
        high, low = split(part)
        proj_out[pl.ds(j, 128, stride=3), :] = nn(columns, high) + nn(columns, low)


def body(
    features,
    conv_weight,
    clip_frames,
    clip_group,
    clip_offset,
    clip_times,
    noise_tokens,
    embed_weight,
    attention_proj,
    norm_gains,
    cotangent,
):
    dma = pltpu.SemaphoreType.DMA
    vm = pltpu.VMEM
    in_hbm = lambda x: pltpu.with_memory_space_constraint(x, pltpu.HBM)
    noisy, att, grads, norms = pl.pallas_call(
        whole,
        name="whole",
        out_shape=(vm((64, 128), F32), vm((128, 2048), BF), vm((384, 128), F32), vm((2, 128), F32)),
        in_specs=[pl.BlockSpec(memory_space=pltpu.HBM)] * 11,
        out_specs=[pl.BlockSpec(memory_space=vm)] * 4,
        scratch_shapes=[
            vm((512, 512), BF), vm((432, 512), BF), vm((3, 1, 32), jnp.int32), vm((1, 32), F32), vm((64, 128), BF),
            vm((64, 2048), BF), vm((3, 2048, 128), BF), vm((2, 128), F32),
            vm((8, 128), F32), vm((4, 512, 128), F32), vm((512, 512), BF), vm((432, 512), F32),
            vm((2, 32, 128), F32), vm((2, 32, 128), F32), vm((64, 128), F32),
            vm((2, 32, 128), F32), vm((2, 32, 128), F32), vm((1, 64, 128), F32), vm((64, 2048), BF),
            vm((64, 2048), BF), vm((2048, 128), BF), vm((128, 384), BF),
            vm((2048, 256), BF), vm((2048, 256), BF), vm((128, 2048), BF), vm((144, 2048), BF),
            vm((2048, 128), F32), vm((2048, 128), F32), vm((2048, 128), F32), vm((2048, 128), F32), vm((256, 2048), BF), vm((256, 2048), BF),
            vm((2048, 128), BF), vm((2048, 128), BF), vm((128, 2048), F32), vm((8, 2048), F32),
            vm((2048, 1024), BF), vm((2048, 1024), BF), vm((2048, 2048), BF), vm((2048, 128), BF), vm((2048, 256), BF), vm((2048, 128), BF),
            vm((N, 8, 128), F32), vm((N, 64, 128), BF), vm((N, 8, 128), F32), vm((N, 16, 128), F32), vm((N, 8, 128), F32),
            dma((10,)), dma((5,)), dma((5,)), dma((N,)), dma((N,)), dma((8,)), dma((8,)), dma((8,)), dma((8,)),
            dma((N,)), dma((N,)), dma((2,)), dma((N,)), dma((N,)), dma((N,)), dma((N,)), dma((N,)), dma((N,)),
            dma((N,)), dma((N,)), dma((N,)), dma((N,)),
        ],
        compiler_params=pltpu.CompilerParams(collective_id=0, has_side_effects=True, vmem_limit_bytes=48 * 2**20),
    )(
        in_hbm(features.reshape(512, 512)),
        in_hbm(conv_weight.reshape(432, 512)),
        in_hbm(clip_frames.reshape(1, 32)),
        in_hbm(clip_group.reshape(1, 32)),
        in_hbm(clip_offset.reshape(1, 32)),
        in_hbm(clip_times.reshape(1, 32)),
        in_hbm(noise_tokens.transpose(0, 2, 1).reshape(64, 128)),
        in_hbm(embed_weight),
        in_hbm(attention_proj.transpose(1, 2, 0, 3).reshape(3, 2048, 128)),
        in_hbm(norm_gains),
        in_hbm(cotangent.reshape(128, 2048)),
    )
    return (
        noisy.reshape(1, 64, 128).transpose(0, 2, 1),
        att.reshape(1, 128, 2048),
        grads.reshape(128, 3, 1, 128),
        norms,
    )


def solution(mesh):
    return jax.shard_map(
        body,
        mesh=mesh,
        in_specs=(
            P("dp", "seq", None, None),
            P(),
            P(),
            P(),
            P(),
            P(),
            P("dp", "seq", None),
            P(),
            P(None, None, "seq", None),
            P(),
            P("dp", "seq", None),
        ),
        out_specs=(P("dp", "seq", None), P("dp", "seq", None), P("dp", None, "seq", None), P()),
        check_vma=False,
    )
```

time: 88.4 us -> 68.1 us (0.77)
  Pallas kernels: 76.4 us -> 64.7 us
  local copies, waits for them, and re-layouts: 8.82 us -> 2.65 us
  other arithmetic: 2 us -> 0 us
    pallas_call x2 -> x1, Pallas kernels: 76.4 us -> 64.7 us  [body(): pl.pallas_call(whole, name='whole', out_shape=(vm((64, 128), F32), vm((12...]
    unnamed x19 -> x4, local copies, waits for them, and re-layouts: 8.25 us -> 2.65 us
    another operation x3 -> x0, other arithmetic: 2 us -> none  [body(): jnp.stack([clip_frames.astype(F32), clip_group.astype(F32), clip_offset.a...]
where the time goes in v2:
time: 68.1 us; the launch traced here: 68 us
  Pallas kernels  64.7 us (95%)
  local copies, waits for them, and re-layouts  2.65 us (4%)
    pallas_call x1, Pallas kernels, body(): pl.pallas_call(whole, name='whole', out_shape=(vm((64, 128), F32), vm((12...  64.7 us
    unnamed x4, local copies, waits for them, and re-layouts  2.65 us

profile of v2, /device:TPU:1, one launch (start us, length us, event | category | flops | bytes accessed | tf_op | source)
XLA Modules:
  0.0 68.0 jit_solution(680419445867837732)
XLA Ops:
  0.6 64.7 %whole.1 = (f32[64,128]{1,0:T(8,128)S(1)}, bf16[128,2048]{1,0:T(8,128)(2,1)S(1)}, f32[384,128]{1,0:T(8,128)S(1)}, f32[2,128]{1,0:T(2,128)S(1)}) custom-call(bf16[512,512]{1,0:T(8,128)(2,1)} %bitcast.24, bf16[432,512]{1,0:T(8,128)(2,1)} %bitcast.26, s32[1,32]{1,0:T(1,128)} %bitcast.28, s32[1,32]{1,0:T(1,128)} %bitcast.29, s32[1,32]{1,0:T(1,128)} %bitcast.30, ...), custom_call_target="tpu_custom_call" | custom-call | tf_op jit(solution)/shard_map/whole/pallas_call | solution.py:524
  65.3 0.6 copy.23
  65.9 0.8 %copy.24 = bf16[1,128,2048]{2,1,0:T(8,128)(2,1)} copy(bf16[1,128,2048]{2,1,0:T(8,128)(2,1)S(1)} %bitcast.20) | data formatting | bytes 1048576
  66.7 0.6 copy.26
  67.3 0.7 copy.25

commit v3 on v2

--- a/solution.py
+++ b/solution.py
@@ -85,10 +85,10 @@
     noisy, att, proj_out, norm_out,
     feat, wconv, ints, times_v, noise, embed, proj, gains,
     tab, actf, actp, conv, edge_out, late_out, own_late, edge_in, late_in, own_late_in, gath,
-    tokens, incoming, ew, keys, vals, keys_t, vals_t, xq, xk, rq, rk, qx, gx, q_n, up_n, out_t, inv, even, odd, dss, dxq, dkv, outs,
-    parts_kv, parts_q, landed_kv, sums, norms,
+    tokens, incoming, ew, keys, vals, keys_t, vals_t, xq, xk, rq, rk, qx, gx, q_n, up_n, out_t, inv, even, odd, dss, dxq, dks, dvs, outs,
+    parts, sums, norms,
     in_sem, edge_send, edge_recv, dp_send, dp_recv, z_send, z_recv, sib_send, sib_recv,
-    cot_send, cot_recv, own_sem, att_send, att_recv, kv_send, kv_recv, q_send, q_recv,
+    cot_send, cot_recv, own_sem, att_send, att_recv, q_send, q_recv, k_send, k_recv, v_send, v_recv,
     nrm_send, nrm_recv, ag_send, ag_recv,
 ):
     slab = lax.axis_index("dp")
@@ -427,57 +427,68 @@
         mean = jnp.mean(x * scaled, axis=1, keepdims=True)
         return (r * (scaled - x * (r * r * mean))).astype(BF)
 
-    def key_block(i, total):
-        at = block_of(i, 256)
+    def score_back(i, _):
+        at = block_of(i, 512)
         for c in range(4):
             qc = pl.ds(c * 512, 512)
             e = (even, odd)[c // 2][at, c % 2 * 512 : c % 2 * 512 + 512]
             dss[at, qc] = (e.astype(F32) * nn(vals[at, :], gx[:, qc])).astype(BF)
-        dkv[at, 128:256] = (nn(even[at, :], up_n[0:1024, :]) + nn(odd[at, :], up_n[1024:2048, :])).astype(BF)
-        grad = nn(dss[at, :], q_n[...]) * LN2
-        x, r = xk[at, :], rk[at, :]
-        dkv[at, 0:128] = rms_back(x, r, gain_k, grad)
+        return 0
+
+    def query_back(i, total):
+        at = block_of(i, 1024)
+        grad = nn(keys_t[...], dss[:, at]).T * scale
+        x, r = xq[at, :], rq[at, :]
+        back = rms_back(x, r, gain_q, grad)
+        for n in range(1024 // 256):
+            place_n = i * 4 + n
+            block = lax.rem(place_n, 4) * 2 + lax.div(place_n, 4)
+            dxq[block_of(lax.rem(chip + block, 8), 256), :] = back[n * 256 : n * 256 + 256, :]
         return total + jnp.sum(grad * x * r, axis=0, keepdims=True)
 
-    norm_k = lax.fori_loop(0, 8, key_block, jnp.zeros((1, 128), F32))
-    part = nn(tokens[...], dkv[...])
-    for j in range(N):
-        parts_kv[j] = part[j // 2 * 8 : j // 2 * 8 + 8, j % 2 * 128 : j % 2 * 128 + 128]
-    landed_kv[slab] = parts_kv[slab]
-    kv_wait = to_all(
-        lambda k: remote(
-            parts_kv.at[peer("dp", k)], landed_kv.at[slab], kv_send.at[k], kv_recv.at[k], dp=peer("dp", k)
-        )
-    )
-
+    def value_back(i, _):
+        at = block_of(i, 1024)
+        dvs[at, :] = (nn(even[at, :], up_n[0:1024, :]) + nn(odd[at, :], up_n[1024:2048, :])).astype(BF)
+        return 0
+
+    def key_back(i, _):
+        at = block_of(i, 1024)
+        dks[at, :] = rms_back(xk[at, :], rk[at, :], gain_k, nn(dss[at, :], q_n[...]) * LN2)
+        return 0
+
+    def share(j, grads, send, recv):
+        parts[j, slab] = nn(tokens[...], grads[...]).astype(BF)
+        mine = parts.at[j, slab]
+        return to_all(lambda k: remote(mine, mine, send.at[k], recv.at[k], dp=peer("dp", k)))
+
+    lax.fori_loop(0, 4, score_back, 0)
+    norm_q = lax.fori_loop(0, 2, query_back, jnp.zeros((1, 128), F32))
     line = iota((8, 128), 0)
-    norms[row] = jnp.where(line == 0, norm_k * gain_k / gain_q, jnp.where(line == 1, norm_k, 0.0))
+    norms[row] = jnp.where(line == 0, norm_q, jnp.where(line == 1, norm_q * gain_q / gain_k, 0.0))
     norm_wait = to_all(
         lambda k: remote(norms.at[row], norms.at[row], nrm_send.at[k], nrm_recv.at[k], seq=peer("seq", k))
     )
-
-    def query_back(i, _):
-        at = place(i)
-        grad = nn(keys_t[...], dss[:, at]).T * scale
-        dxq[block_of(lax.rem(chip + i, 8), 256), :] = rms_back(xq[at, :], rq[at, :], gain_q, grad)
-        return 0
-
-    lax.fori_loop(0, 8, query_back, 0)
-    parts_q[slab] = nn(tokens[...], dxq[...]).astype(BF)
-    q_wait = to_all(
-        lambda k: remote(parts_q.at[slab], parts_q.at[slab], q_send.at[k], q_recv.at[k], dp=peer("dp", k))
-    )
-    columns = embed[:, block_of(slab)].astype(F32).T.astype(BF)
-    kv_wait()
+    q_wait = share(0, dxq, q_send, q_recv)
+    lax.fori_loop(0, 2, value_back, 0)
+    v_wait = share(2, dvs, v_send, v_recv)
+    lax.fori_loop(0, 2, key_back, 0)
+    k_wait = share(1, dks, k_send, k_recv)
     norm_wait()
-    for i, buffer in enumerate((landed_kv, norms)):
-        total = buffer[0]
-        for j in range(1, N):
-            total = total + buffer[j]
-        sums[slab, i * 8 : i * 8 + 8, :] = total
+    norm = norms[0]
+    for j in range(1, N):
+        norm = norm + norms[j]
+    sums[slab] = norm
     ag_wait = to_all(
         lambda k: remote(sums.at[slab], sums.at[slab], ag_send.at[k], ag_recv.at[k], dp=peer("dp", k))
     )
+    columns = embed[:, block_of(slab)].astype(F32).T.astype(BF)
+
+    def project(j):
+        whole_sum = parts[j, 0].astype(F32)
+        for i in range(1, N):
+            whole_sum = whole_sum + parts[j, i].astype(F32)
+        high, low = split(whole_sum)
+        proj_out[pl.ds(j, 128, stride=3), :] = nn(columns, high) + nn(columns, low)
 
     def out_wait(p, _):
         @pl.when(p != row)
@@ -490,19 +501,16 @@
     lax.fori_loop(0, N, out_wait, 0)
     own_out.wait()
     q_wait()
-    whole_q = parts_q[0].astype(F32)
+    project(0)
+    v_wait()
+    project(2)
+    k_wait()
+    project(1)
+    ag_wait()
+    norm = sums[0]
     for j in range(1, N):
-        whole_q = whole_q + parts_q[j].astype(F32)
-    ag_wait()
-    whole_k = jnp.concatenate([sums[2 * b, 0:8, :] for b in range(8)], axis=0)
-    whole_v = jnp.concatenate([sums[2 * b + 1, 0:8, :] for b in range(8)], axis=0)
-    norm = sums[0, 8:16, :]
-    for j in range(1, N):
-        norm = norm + sums[j, 8:16, :]
+        norm = norm + sums[j]
     norm_out[...] = norm[0:2, :]
-    for j, part in enumerate((whole_q, whole_k, whole_v)):
-        high, low = split(part)
-        proj_out[pl.ds(j, 128, stride=3), :] = nn(columns, high) + nn(columns, low)
 
 
 def body(
@@ -537,11 +545,11 @@
             vm((2048, 256), BF), vm((2048, 256), BF), vm((128, 2048), BF), vm((144, 2048), BF),
             vm((2048, 128), F32), vm((2048, 128), F32), vm((2048, 128), F32), vm((2048, 128), F32), vm((256, 2048), BF), vm((256, 2048), BF),
             vm((2048, 128), BF), vm((2048, 128), BF), vm((128, 2048), F32), vm((8, 2048), F32),
-            vm((2048, 1024), BF), vm((2048, 1024), BF), vm((2048, 2048), BF), vm((2048, 128), BF), vm((2048, 256), BF), vm((2048, 128), BF),
-            vm((N, 8, 128), F32), vm((N, 64, 128), BF), vm((N, 8, 128), F32), vm((N, 16, 128), F32), vm((N, 8, 128), F32),
+            vm((2048, 1024), BF), vm((2048, 1024), BF), vm((2048, 2048), BF), vm((2048, 128), BF), vm((2048, 128), BF), vm((2048, 128), BF), vm((2048, 128), BF),
+            vm((3, N, 64, 128), BF), vm((N, 8, 128), F32), vm((N, 8, 128), F32),
             dma((10,)), dma((5,)), dma((5,)), dma((N,)), dma((N,)), dma((8,)), dma((8,)), dma((8,)), dma((8,)),
             dma((N,)), dma((N,)), dma((2,)), dma((N,)), dma((N,)), dma((N,)), dma((N,)), dma((N,)), dma((N,)),
-            dma((N,)), dma((N,)), dma((N,)), dma((N,)),
+            dma((N,)), dma((N,)), dma((N,)), dma((N,)), dma((N,)), dma((N,)),
         ],
         compiler_params=pltpu.CompilerParams(collective_id=0, has_side_effects=True, vmem_limit_bytes=48 * 2**20),
     )(

time: 68.1 us -> 65.6 us (0.963)
  Pallas kernels: 64.7 us -> 62.2 us
    pallas_call x1, Pallas kernels: 64.7 us -> 62.2 us  [body(): pl.pallas_call(whole, name='whole', out_shape=(vm((64, 128), F32), vm((12...]
where the time goes in v3:
time: 65.6 us; the launch traced here: 65.5 us
  Pallas kernels  62.2 us (95%)
  local copies, waits for them, and re-layouts  2.65 us (4%)
    pallas_call x1, Pallas kernels, body(): pl.pallas_call(whole, name='whole', out_shape=(vm((64, 128), F32), vm((12...  62.2 us
    unnamed x4, local copies, waits for them, and re-layouts  2.65 us

profile of v3, /device:TPU:1, one launch (start us, length us, event | category | flops | bytes accessed | tf_op | source)
XLA Modules:
  0.0 65.5 jit_solution(7550550514587597603)
XLA Ops:
  0.6 62.2 %whole.1 = (f32[64,128]{1,0:T(8,128)S(1)}, bf16[128,2048]{1,0:T(8,128)(2,1)S(1)}, f32[384,128]{1,0:T(8,128)S(1)}, f32[2,128]{1,0:T(2,128)S(1)}) custom-call(bf16[512,512]{1,0:T(8,128)(2,1)} %bitcast.24, bf16[432,512]{1,0:T(8,128)(2,1)} %bitcast.26, s32[1,32]{1,0:T(1,128)} %bitcast.28, s32[1,32]{1,0:T(1,128)} %bitcast.29, s32[1,32]{1,0:T(1,128)} %bitcast.30, ...), custom_call_target="tpu_custom_call" | custom-call | tf_op jit(solution)/shard_map/whole/pallas_call | solution.py:532
  62.9 0.6 copy.23
  63.5 0.8 %copy.24 = bf16[1,128,2048]{2,1,0:T(8,128)(2,1)} copy(bf16[1,128,2048]{2,1,0:T(8,128)(2,1)S(1)} %bitcast.20) | data formatting | bytes 1048576
  64.3 0.6 copy.26
  64.9 0.7 %copy.25 = f32[128,3,1,128]{3,2,1,0:T(1,128)} copy(f32[128,3,1,128]{3,2,1,0:T(1,128)S(1)} %bitcast.21) | data formatting | bytes 393216

commit v4 on v3

--- a/solution.py
+++ b/solution.py
@@ -428,7 +428,7 @@
         return (r * (scaled - x * (r * r * mean))).astype(BF)
 
     def score_back(i, _):
-        at = block_of(i, 512)
+        at = block_of(i, 1024)
         for c in range(4):
             qc = pl.ds(c * 512, 512)
             e = (even, odd)[c // 2][at, c % 2 * 512 : c % 2 * 512 + 512]
@@ -461,7 +461,7 @@
         mine = parts.at[j, slab]
         return to_all(lambda k: remote(mine, mine, send.at[k], recv.at[k], dp=peer("dp", k)))
 
-    lax.fori_loop(0, 4, score_back, 0)
+    lax.fori_loop(0, 2, score_back, 0)
     norm_q = lax.fori_loop(0, 2, query_back, jnp.zeros((1, 128), F32))
     line = iota((8, 128), 0)
     norms[row] = jnp.where(line == 0, norm_q, jnp.where(line == 1, norm_q * gain_q / gain_k, 0.0))

time: 65.6 us -> 65.2 us (level)
  no operation moved by 1% of the time
where the time goes in v4:
time: 65.2 us; the launch traced here: 65.1 us
  Pallas kernels  61.8 us (95%)
  local copies, waits for them, and re-layouts  2.65 us (4%)
    pallas_call x1, Pallas kernels, body(): pl.pallas_call(whole, name='whole', out_shape=(vm((64, 128), F32), vm((12...  61.8 us
    unnamed x4, local copies, waits for them, and re-layouts  2.65 us

profile of v4, /device:TPU:1, one launch (start us, length us, event | category | flops | bytes accessed | tf_op | source)
XLA Modules:
  0.0 65.1 jit_solution(15674124588612456047)
XLA Ops:
  0.6 61.8 %whole.1 = (f32[64,128]{1,0:T(8,128)S(1)}, bf16[128,2048]{1,0:T(8,128)(2,1)S(1)}, f32[384,128]{1,0:T(8,128)S(1)}, f32[2,128]{1,0:T(2,128)S(1)}) custom-call(bf16[512,512]{1,0:T(8,128)(2,1)} %bitcast.24, bf16[432,512]{1,0:T(8,128)(2,1)} %bitcast.26, s32[1,32]{1,0:T(1,128)} %bitcast.28, s32[1,32]{1,0:T(1,128)} %bitcast.29, s32[1,32]{1,0:T(1,128)} %bitcast.30, ...), custom_call_target="tpu_custom_call" | custom-call | tf_op jit(solution)/shard_map/whole/pallas_call | solution.py:532
  62.5 0.6 copy.23
  63.1 0.8 %copy.24 = bf16[1,128,2048]{2,1,0:T(8,128)(2,1)} copy(bf16[1,128,2048]{2,1,0:T(8,128)(2,1)S(1)} %bitcast.20) | data formatting | bytes 1048576
  63.9 0.6 copy.26
  64.5 0.7 %copy.25 = f32[128,3,1,128]{3,2,1,0:T(1,128)} copy(f32[128,3,1,128]{3,2,1,0:T(1,128)S(1)} %bitcast.21) | data formatting | bytes 393216

commit v5 on v4

--- a/solution.py
+++ b/solution.py
@@ -188,11 +188,6 @@
         for ob in range(2):
             at = slice(ob * 16, ob * 16 + 16)
             edge_out[side, at, :], late_out[side, at, :] = sums_of(out_row, ob)
-    mains = {}
-    for a in range(2):
-        for ob in range(2):
-            at = slice((a * 2 + ob) * 16, (a * 2 + ob) * 16 + 16)
-            mains[a, ob], own_late[at, :] = sums_of(a, ob)
     entered()
 
     routes = []
@@ -214,8 +209,14 @@
         remote(own_late, own_late_in.at[0], edge_send.at[4], edge_recv.at[4], dp=peer("dp", 1)),
         slab < N - 1, slab > 0, own_late_in, 0,
     ))
-    for copy, goes, _, _, _ in routes:
+    for copy, goes, _, _, _ in routes[:4]:
         pl.when(goes)(copy.start)
+    mains = {}
+    for a in range(2):
+        for ob in range(2):
+            at = slice((a * 2 + ob) * 16, (a * 2 + ob) * 16 + 16)
+            mains[a, ob], own_late[at, :] = sums_of(a, ob)
+    pl.when(routes[4][1])(routes[4][0].start)
     def cot_copy(k):
         return remote(
             cot.at[:, block_of(peer("seq", k))], incoming.at[block_of(row)], cot_send.at[k], cot_recv.at[k],

time: 65.2 us -> 65.2 us (level)
  no operation moved by 1% of the time
where the time goes in v5:
time: 65.2 us; the launch traced here: 65.1 us
  Pallas kernels  61.8 us (95%)
  local copies, waits for them, and re-layouts  2.65 us (4%)
    pallas_call x1, Pallas kernels, body(): pl.pallas_call(whole, name='whole', out_shape=(vm((64, 128), F32), vm((12...  61.8 us
    unnamed x4, local copies, waits for them, and re-layouts  2.65 us

profile of v5, /device:TPU:1, one launch (start us, length us, event | category | flops | bytes accessed | tf_op | source)
XLA Modules:
  0.0 65.1 jit_solution(9131328218546196356)
XLA Ops:
  0.6 61.8 %whole.1 = (f32[64,128]{1,0:T(8,128)S(1)}, bf16[128,2048]{1,0:T(8,128)(2,1)S(1)}, f32[384,128]{1,0:T(8,128)S(1)}, f32[2,128]{1,0:T(2,128)S(1)}) custom-call(bf16[512,512]{1,0:T(8,128)(2,1)} %bitcast.24, bf16[432,512]{1,0:T(8,128)(2,1)} %bitcast.26, s32[1,32]{1,0:T(1,128)} %bitcast.28, s32[1,32]{1,0:T(1,128)} %bitcast.29, s32[1,32]{1,0:T(1,128)} %bitcast.30, ...), custom_call_target="tpu_custom_call" | custom-call | tf_op jit(solution)/shard_map/whole/pallas_call | solution.py:533
  62.5 0.6 copy.23
  63.1 0.8 %copy.24 = bf16[1,128,2048]{2,1,0:T(8,128)(2,1)} copy(bf16[1,128,2048]{2,1,0:T(8,128)(2,1)S(1)} %bitcast.20) | data formatting | bytes 1048576
  63.9 0.6 copy.26
  64.4 0.7 %copy.25 = f32[128,3,1,128]{3,2,1,0:T(1,128)} copy(f32[128,3,1,128]{3,2,1,0:T(1,128)S(1)} %bitcast.21) | data formatting | bytes 393216
